TPU v7x, 256 devices: a whole 4x4x8 slice. The times are simulated.
256 devices in a mesh: tensor: 16 (over z, core), context: 16 (over y, x).
Axes of the slice: x: 4, y: 4, z: 8, core: 2. Of those that a mesh axis runs over, the one named last changes fastest.
Arguments:
- hidden: bfloat16 [4096, 8192], P(('context', 'tensor')), may hold values from -6 to 6
- w_proj: bfloat16 [8192, 12288], P(None, 'tensor'), may hold values from -0.0625 to 0.0625
- w_dt: bfloat16 [128, 8192], P('tensor'), may hold values from -0.0625 to 0.0625
- dt_bias: float32 [128], P('tensor'), may hold values from -9 to -3
- a_log: float32 [128], P('tensor'), may hold values from 0 to 0.6
- d_skip: float32 [128], P('tensor'), may hold values from 0.5 to 1.5
- doc_lengths: int32 [8], replicated, may hold values from 1 to 1920, as said below
- grad_out: bfloat16 [4096, 8192], P('context', 'tensor'), may hold values from -3 to 3
Outputs:
- ssd_out: bfloat16 [4096, 8192], P('context', 'tensor')
- grad_hidden: bfloat16 [4096, 8192], P(('context', 'tensor'))
Inputs may be any that keep to these rules, and one draw needn't show every extreme that they name: `doc_lengths`: the 8 lengths sum to 4096; the first document has exactly 1920 tokens and the second exactly 448.
All inputs are finite; a program needn't handle non-finite values.
Results may differ from a plain program's by a relative error of at most 0.029.
Values may be sent and summed in bfloat16 or wider, within the bound.
A program may use at most 128 MiB of HBM per device.

v0:
```python
import jax
import jax.numpy as jnp
from jax import lax
from jax.sharding import PartitionSpec as P

HEAD_DIM = 64
BLOCK_LEN = 128
MX_BLOCK = 32


PRECISE = lax.Precision.HIGHEST


def entering(part, axis, combine, identity, reverse):
    count = lax.axis_size(axis)
    place = lax.axis_index(axis)
    ahead = count - 1 - place if reverse else place
    gathered = jax.tree.map(lambda a: lax.all_gather(a, axis), part)
    state = jax.tree.map(lambda a, e: jnp.zeros_like(a) + jnp.asarray(e, a.dtype), part, identity)

    def one(lap, state):
        source = count - 1 - lap if reverse else lap
        return combine(
            state, jax.tree.map(lambda a: lax.dynamic_index_in_dim(a, source, 0, False), gathered)
        )

    return lax.fori_loop(0, ahead, one, state)


def block_encode(rows):
    row_total = rows.shape[0]
    feat_width = rows.shape[1]
    values = rows.astype(jnp.float32).reshape(row_total, feat_width // MX_BLOCK, MX_BLOCK)
    largest = jnp.max(jnp.abs(values), axis=2)
    scale_power = jnp.full(largest.shape, 2.0 ** (-48), jnp.float32)
    for exponent in range(-39, 40):
        scale_power = jnp.where(largest >= 2.0**exponent, 2.0 ** (exponent - 8), scale_power)
    scaled = values / scale_power[:, :, None]
    magnitude = jnp.abs(scaled)
    quantum = jnp.full(scaled.shape, 2.0 ** (-9), jnp.float32)
    for exponent in range(-5, 9):
        quantum = jnp.where(magnitude >= 2.0**exponent, 2.0 ** (exponent - 3), quantum)
    step_ratio = scaled / quantum
    floored = jnp.floor(step_ratio)
    remainder = step_ratio - floored
    parity = floored - 2.0 * jnp.floor(0.5 * floored)
    upward = (remainder > 0.5) | (remainder == 0.5) & (parity == 1.0)
    snapped = (floored + jnp.where(upward, 1.0, 0.0)) * quantum
    snapped = jnp.clip(snapped, -448.0, 448.0)
    return (
        snapped.reshape(row_total, feat_width).astype(jnp.bfloat16),
        scale_power.astype(jnp.bfloat16),
    )


def dequantize(elements, scale_power):
    row_total = elements.shape[0]
    feat_width = elements.shape[1]
    blocks_view = elements.astype(jnp.float32).reshape(row_total, feat_width // MX_BLOCK, MX_BLOCK)
    restored = blocks_view * scale_power.astype(jnp.float32)[:, :, None]
    return restored.reshape(row_total, feat_width).astype(jnp.bfloat16)


def segment_index(positions, doc_lengths):
    starts = jnp.cumsum(doc_lengths) - doc_lengths
    inside = (starts[None, :] <= positions[:, None]).astype(jnp.int32)
    return jnp.sum(inside, axis=1) - 1


def block_parts(x_heads, b_rows, c_rows, dt_rows, decay_rates, segments, previous):
    cumulative = jnp.cumsum(dt_rows * decay_rates[None], axis=0)
    positions = jnp.arange(segments.shape[0])
    allowed = (positions[:, None] >= positions[None, :]) & (segments[:, None] == segments[None, :])
    allowed_grid = allowed[:, :, None, None]
    log_gap = cumulative[:, None] - cumulative[None, :]
    decay_grid = jnp.where(allowed_grid, jnp.exp(jnp.where(allowed_grid, log_gap, 0.0)), 0.0)
    scores = jnp.einsum("tgn,sgn->tsg", c_rows, b_rows, precision=PRECISE)
    mixing = scores[:, :, :, None] * decay_grid * dt_rows[None]
    inner_out = jnp.einsum("tsge,sgep->tgep", mixing, x_heads, precision=PRECISE)
    continues = (segments == previous).astype(jnp.float32)
    carry_weight = jnp.exp(cumulative) * continues[:, None, None]
    in_last = (segments == segments[-1]).astype(jnp.float32)
    keep_weight = jnp.exp(cumulative[-1][None] - cumulative) * dt_rows * in_last[:, None, None]
    end_state = jnp.einsum("sge,sgep,sgn->gepn", keep_weight, x_heads, b_rows, precision=PRECISE)
    block_decay = jnp.exp(cumulative[-1]) * continues[-1]
    return (inner_out, carry_weight, block_decay, end_state)


def summarize(decay_all, state_all):
    running_decay = jnp.ones_like(decay_all[0])
    running_state = jnp.zeros_like(state_all[0])
    for block_index in range(decay_all.shape[0]):
        running_state = (
            decay_all[block_index][:, :, None, None] * running_state + state_all[block_index]
        )
        running_decay = running_decay * decay_all[block_index]
    return (running_decay, running_state)


def assemble(inner_all, weight_all, decay_all, state_all, cmat_all, state_in):
    results = []
    current = state_in
    for block_index in range(inner_all.shape[0]):
        carried = jnp.einsum("tgn,gepn->tgep", cmat_all[block_index], current, precision=PRECISE)
        results.append(inner_all[block_index] + carried * weight_all[block_index][:, :, :, None])
        current = decay_all[block_index][:, :, None, None] * current + state_all[block_index]
    joined = jnp.concatenate(results, axis=0)
    return joined.reshape(joined.shape[0], joined.shape[2] * joined.shape[3])


def chain_combine(earlier, later):
    return (earlier[0] * later[0], later[0][:, :, None, None] * earlier[1] + later[1])


def per_device(hidden, w_proj, w_dt, dt_bias, a_log, d_skip, doc_lengths, grad_out):
    heads_here = w_dt.shape[0]
    x_width = heads_here * HEAD_DIM
    state_width = (w_proj.shape[1] - x_width) // 2
    elements, scale_power = block_encode(hidden)
    gathered = (
        lax.all_gather(elements, "tensor", axis=0, tiled=True),
        lax.all_gather(scale_power, "tensor", axis=0, tiled=True),
    )
    quantized = dequantize(gathered[0], gathered[1])
    span_rows = quantized.shape[0]
    blocks = span_rows // BLOCK_LEN
    projected = jnp.dot(quantized, w_proj, preferred_element_type=jnp.float32).astype(jnp.bfloat16)
    dt_raw = lax.dot_general(
        quantized, w_dt, (((1,), (1,)), ((), ())), preferred_element_type=jnp.float32
    )
    my_index = lax.axis_index("context")
    positions = my_index * span_rows + jnp.arange(span_rows, dtype=jnp.int32)
    segments = segment_index(positions, doc_lengths)
    previous_segs = segment_index(positions[::BLOCK_LEN] - 1, doc_lengths)
    decay_rates = (-jnp.exp(a_log)).reshape(1, heads_here)
    skip_gain = d_skip.reshape(1, heads_here)

    def local_parts(proj_values, dt_values):
        x_heads = jax.nn.silu(proj_values[:, :x_width]).reshape(span_rows, 1, heads_here, HEAD_DIM)
        b_rows = jax.nn.silu(proj_values[:, x_width : x_width + state_width]).reshape(
            span_rows, 1, state_width
        )
        c_rows = jax.nn.silu(proj_values[:, x_width + state_width :]).reshape(
            span_rows, 1, state_width
        )
        dt_rows = jax.nn.softplus(dt_values + dt_bias[None]).reshape(span_rows, 1, heads_here)
        inner_list, weight_list, decay_list, state_list, cmat_list = ([], [], [], [], [])
        for block_index in range(blocks):
            first_row = block_index * BLOCK_LEN
            last_row = first_row + BLOCK_LEN
            inner_out, carry_weight, block_decay, end_state = block_parts(
                x_heads[first_row:last_row],
                b_rows[first_row:last_row],
                c_rows[first_row:last_row],
                dt_rows[first_row:last_row],
                decay_rates,
                segments[first_row:last_row],
                previous_segs[block_index],
            )
            inner_list.append(inner_out + skip_gain[None, :, :, None] * x_heads[first_row:last_row])
            weight_list.append(carry_weight)
            decay_list.append(block_decay)
            state_list.append(end_state)
            cmat_list.append(c_rows[first_row:last_row])
        return (
            jnp.stack(inner_list),
            jnp.stack(weight_list),
            jnp.stack(decay_list),
            jnp.stack(state_list),
            jnp.stack(cmat_list),
        )

    parts, parts_back = jax.vjp(local_parts, projected.astype(jnp.float32), dt_raw)
    (total_decay, total_state), summary_back = jax.vjp(summarize, parts[2], parts[3])
    identity = (jnp.ones_like(total_decay), jnp.zeros_like(total_state))
    incoming = entering((total_decay, total_state), "context", chain_combine, identity, False)[1]
    ssd_y, assemble_back = jax.vjp(
        assemble, parts[0], parts[1], parts[2], parts[3], parts[4], incoming
    )
    assemble_grads = assemble_back(grad_out.astype(jnp.float32))
    from_outputs = assemble_grads[5]
    returned = entering((total_decay, from_outputs), "context", chain_combine, identity, True)[1]
    decay_grad = jnp.sum(returned * incoming, axis=(2, 3))
    summary_grads = summary_back((decay_grad, returned))
    part_grads = (
        assemble_grads[0],
        assemble_grads[1],
        assemble_grads[2] + summary_grads[0],
        assemble_grads[3] + summary_grads[1],
        assemble_grads[4],
    )
    proj_values_grad, dt_values_grad = parts_back(part_grads)
    proj_grad = proj_values_grad.astype(jnp.bfloat16)
    dt_grad = dt_values_grad.astype(jnp.bfloat16)
    term = lax.dot_general(
        proj_grad, w_proj, (((1,), (1,)), ((), ())), preferred_element_type=jnp.float32
    )
    grad_hidden = lax.psum_scatter(
        term + jnp.dot(dt_grad, w_dt, preferred_element_type=jnp.float32),
        "tensor",
        scatter_dimension=0,
        tiled=True,
    )
    return (ssd_y.astype(jnp.bfloat16), grad_hidden.astype(jnp.bfloat16))


def solution(mesh):
    placed = (
        P(("context", "tensor"), None),
        P(None, "tensor"),
        P("tensor", None),
        P("tensor"),
        P("tensor"),
        P("tensor"),
        P(),
        P("context", "tensor"),
    )
    return jax.shard_map(
        per_device,
        mesh=mesh,
        in_specs=placed,
        out_specs=(P("context", "tensor"), P(("context", "tensor"), None)),
        check_vma=False,
    )
```

profile of v0, /device:TPU:1, one launch (start us, length us, event | category | flops | bytes accessed | tf_op | source)
XLA Modules:
  0.0 346.2 jit_solution(7039961225603737109)
XLA Ops:
  14.7 2.5 compare_convert_fusion
  18.4 21.7 %all_gather.25 = bf16[256,256]{1,0:T(8,128)(2,1)S(1)} all-gather(bf16[16,256]{1,0:T(8,128)(2,1)S(1)} %get-tuple-element.216), channel_id=1, replica_groups=mesh['tensor'=16,'context'=16] {'tensor'}, dimensions={0}, use_global_device_ids=true | all-gather | bytes 139264 | tf_op jit(solution)/shard_map/all_gather | solution.py:122
  40.2 3.9 %mul.674 = f32[256,256,32]{0,2,1:T(8,128)} broadcast(f32[256,256]{0,1:T(8,128)S(1)} %copy.136), dimensions={0,1} | broadcast | bytes 8650752 | tf_op jit(solution)/shard_map/mul | solution.py:60
  44.1 9.1 %copy.137 = f32[256,8192]{1,0:T(8,128)} copy(f32[256,8192]{0,1:T(8,128)} %bitcast.391) | data formatting | bytes 16777216 | tf_op jit(solution)/shard_map/mul | solution.py:60
  53.5 5.6 %all-gather.6.cloned.1.call-done = bf16[256,8192]{1,0:T(8,128)(2,1)} async-done(((bf16[16,8192]{1,0:T(8,128)(2,1)}), bf16[256,8192]{1,0:T(8,128)(2,1)}) %all-gather.6.cloned.1.call-update) | async-done | bytes 4194320 | tf_op jit(solution)/shard_map/all_gather | solution.py:121
  59.1 6.4 %compare_select_fusion.2 = (f32[256,8]{0,1:T(8,128)S(1)}, f32[256,8]{0,1:T(8,128)}) fusion(f32[8]{0:T(128)S(1)} %copy-done.60, bf16[8,8192]{1,0:T(8,128)(2,1)S(1)} %copy-done, f32[256,8192]{1,0:T(8,128)} %copy.137, bf16[256,8192]{1,0:T(8,128)(2,1)} %all-gather.6.cloned.1.call-done), kind=kOutput, calls=%fused_computation.209 | convolution fusion | flops 39860224 | bytes 12730400 | tf_op jit(solution)/shard_map/dot_general | solution.py:128
  66.2 10.2 %fusion = f32[256,768]{1,0:T(8,128)S(1)} fusion(bf16[8192,768]{1,0:T(8,128)(2,1)} %param.13, f32[256,8192]{1,0:T(8,128)} %copy.137, bf16[256,8192]{1,0:T(8,128)(2,1)} %all-gather.6.cloned.1.call-done), kind=kOutput, calls=%fused_computation.7 | convolution fusion | flops 3227910144 | bytes 25952256 | tf_op jit(solution)/shard_map/dot_general | solution.py:127
  77.9 1.8 broadcast_multiply_fusion
  83.3 17.1 %all_gather.26 = f32[16,1,8]{2,1,0:T(1,128)S(1)} all-gather(f32[1,1,8]{2,1,0:T(1,128)S(1)} %copy.146), channel_id=1, replica_groups=mesh['tensor'=16,'context'=16] {'context'}, dimensions={0}, use_global_device_ids=true | all-gather | bytes 544 | tf_op jit(solution)/shard_map/all_gather | solution.py:18
  100.4 36.3 %all-gather.10.cloned.1.call-done = f32[128,64,128]{2,1,0:T(8,128)} async-done(((f32[8,64,128]{2,1,0:T(8,128)}), f32[128,64,128]{2,1,0:T(8,128)}) %all-gather.10.cloned.1.call-update) | async-done | bytes 4194320 | tf_op jit(solution)/shard_map/all_gather | solution.py:18
  136.7 16.8 %while.27 = (s32[]{:T(128)}, f32[1,8,64,128]{3,2,1,0:T(8,128)S(1)}, s32[]{:T(128)}, f32[16,1,8]{2,1,0:T(1,128)S(1)}, f32[16,1,8,64,128]{4,3,2,1,0:T(8,128)}, /*index=5*/s32[]{:T(128)}, s32[]{:T(128)}, s32[]{:T(128)}, s32[]{:T(128)}) while((s32[]{:T(128)}, f32[1,8,64,128]{3,2,1,0:T(8,128)S(1)}, s32[]{:T(128)}, f32[16,1,8]{2,1,0:T(1,128)S(1)}, ...), condition=%wide.region_11.12_spmd, body=%wide.region_10.11_spmd.sunk | while | flops 131078 | bytes 786675 | solution.py:27
  158.7 2.1 fusion.19
  163.8 1.8 convolution_add_fusion.2
  171.8 2.8 fusion.25
  175.7 2.8 fusion.27
  179.6 1.9 fusion.10
  181.5 1.9 fusion.9
  183.5 35.5 %all-gather.8.cloned.1.call-done = f32[128,64,128]{2,1,0:T(8,128)} async-done(((f32[8,64,128]{2,1,0:T(8,128)}), f32[128,64,128]{2,1,0:T(8,128)}) %all-gather.8.cloned.1.call-update) | async-done | bytes 4194320 | tf_op jit(solution)/shard_map/all_gather | solution.py:18
  220.1 1.9 multiply_reduce_fusion.6
  222.0 2.0 multiply_reduce_fusion.7
  233.9 6.6 %fusion.23 = f32[256,8192]{1,0:T(8,128)S(1)} fusion(bf16[8192,768]{1,0:T(8,128)(2,1)} %param.13, f32[256,512]{1,0:T(8,128)} %get-tuple-element.220, f32[256,128]{1,0:T(8,128)S(1)} %get-tuple-element.219, f32[256,128]{1,0:T(8,128)S(1)} %get-tuple-element.218), kind=kOutput, calls=%fused_computation.78 | convolution fusion | flops 3221815296 | bytes 21757952 | tf_op jit(solution)/shard_map/dot_general | solution.py:195
  240.7 4.6 %convolution_add_fusion = f32[256,8192]{1,0:T(8,128)} fusion(f32[256,8192]{1,0:T(8,128)S(1)} %fusion.23, bf16[8,8192]{1,0:T(8,128)(2,1)S(1)} %copy-done, f32[256,8]{0,1:T(8,128)S(1)} %copy-done.27, f32[128,1,8]{0,2,1:T(8,128)S(1)} %get-tuple-element.256, f32[128,1,8]{0,2,1:T(8,128)S(1)} %get-tuple-element.255), kind=kOutput, calls=%fused_computation.4 | convolution fusion | flops 35680256 | bytes 16924672 | tf_op jit(solution)/shard_map/dot_general | solution.py:199
  249.6 88.3 %reduce-scatter.2.cloned.1.call-done = f32[16,8192]{1,0:T(8,128)} async-done(((f32[256,8192]{1,0:T(8,128)}), f32[16,8192]{1,0:T(8,128)}) %reduce-scatter.2.cloned.1.call-update) | async-done | bytes 524304 | tf_op jit(solution)/shard_map/reduce_scatter | solution.py:198
  337.9 1.8 convert_element_type.76
  (262 shorter events, 62.2 us)
Async XLA Ops:
  7.2 52.0 %copy-start = (bf16[8,8192]{1,0:T(8,128)(2,1)S(1)}, bf16[8,8192]{1,0:T(8,128)(2,1)}, u32[]{:S(2)}) copy-start(bf16[8,8192]{1,0:T(8,128)(2,1)} %param.14) | copy-start | bytes 393220
  7.2 51.9 %all-gather.6.cloned.1.call-start = ((), (), s32[]{:S(2)}) async-start(), calls=%async_computation.1 | async-start | bytes 4456448 | tf_op jit(solution)/shard_map/all_gather | solution.py:121
  12.9 123.8 %all-gather.10.cloned.1.call-start = ((), (), s32[]{:S(2)}) async-start(), calls=%async_computation.4 | async-start | bytes 4456448 | tf_op jit(solution)/shard_map/all_gather | solution.py:18
  17.2 62.5 %copy-start.39 = (f32[128]{0:T(128)}, f32[128]{0:T(128)S(1)}, u32[]{:S(2)}) copy-start(f32[128]{0:T(128)S(1)} %get-tuple-element.249) | copy-start | bytes 1540
  17.2 62.5 %copy-start.41 = (f32[128]{0:T(128)}, f32[128]{0:T(128)S(1)}, u32[]{:S(2)}) copy-start(f32[128]{0:T(128)S(1)} %get-tuple-element.250) | copy-start | bytes 1540
  17.2 62.5 %copy-start.47 = (f32[128]{0:T(128)}, f32[128]{0:T(128)S(1)}, u32[]{:S(2)}) copy-start(f32[128]{0:T(128)S(1)} %get-tuple-element.252) | copy-start | bytes 1540
  17.2 62.5 %copy-start.48 = (f32[128]{0:T(128)}, f32[128]{0:T(128)S(1)}, u32[]{:S(2)}) copy-start(f32[128]{0:T(128)S(1)} %get-tuple-element.251) | copy-start | bytes 1540
  76.5 102.0 %copy-start.1 = (f32[256,128]{1,0:T(8,128)}, f32[256,128]{1,0:T(8,128)S(1)}, u32[]{:S(2)}) copy-start(f32[256,128]{1,0:T(8,128)S(1)} %get-tuple-element.223) | copy-start | bytes 393220
  79.7 76.9 %copy-start.44 = (f32[8]{0:T(128)}, f32[8]{0:T(128)S(1)}, u32[]{:S(2)}) copy-start(f32[8]{0:T(128)S(1)} %get-tuple-element.265) | copy-start | bytes 100
  79.8 76.8 %copy-start.25 = (f32[128,8]{0,1:T(8,128)}, f32[128,8]{0,1:T(8,128)S(1)}, u32[]{:S(2)}) copy-start(f32[128,8]{0,1:T(8,128)S(1)} %get-tuple-element.235) | copy-start | bytes 12292
  79.8 76.8 %copy-start.26 = (f32[128,8]{0,1:T(8,128)}, f32[128,8]{0,1:T(8,128)S(1)}, u32[]{:S(2)}) copy-start(f32[128,8]{0,1:T(8,128)S(1)} %get-tuple-element.236) | copy-start | bytes 12292
  79.8 76.8 %copy-start.50 = (f32[128,8]{0,1:T(8,128)}, f32[128,8]{0,1:T(8,128)S(1)}, u32[]{:S(2)}) copy-start(f32[128,8]{0,1:T(8,128)S(1)} %get-tuple-element.237) | copy-start | bytes 12292
  79.8 76.8 %copy-start.52 = (f32[128,8]{0,1:T(8,128)}, f32[128,8]{0,1:T(8,128)S(1)}, u32[]{:S(2)}) copy-start(f32[128,8]{0,1:T(8,128)S(1)} %get-tuple-element.234) | copy-start | bytes 12292
  81.3 137.7 %all-gather.8.cloned.1.call-start = ((), (), s32[]{:S(2)}) async-start(), calls=%async_computation.3 | async-start | bytes 4456448 | tf_op jit(solution)/shard_map/all_gather | solution.py:18
  81.5 75.1 %copy-start.33 = (pred[128,128]{1,0:T(8,128)(4,1)}, pred[128,128]{1,0:T(8,128)(4,1)S(1)}, u32[]{:S(2)}) copy-start(pred[128,128]{1,0:T(8,128)(4,1)S(1)} %get-tuple-element.266) | copy-start | bytes 49156
  81.5 75.1 %copy-start.35 = (pred[128,128]{1,0:T(8,128)(4,1)}, pred[128,128]{1,0:T(8,128)(4,1)S(1)}, u32[]{:S(2)}) copy-start(pred[128,128]{1,0:T(8,128)(4,1)S(1)} %get-tuple-element.267) | copy-start | bytes 49156
  82.9 73.7 %copy-start.17 = (f32[128,128]{1,0:T(8,128)}, f32[128,128]{1,0:T(8,128)S(1)}, u32[]{:S(2)}) copy-start(f32[128,128]{1,0:T(8,128)S(1)} %copy.150) | copy-start | bytes 196612
  83.2 73.4 %copy-start.19 = (f32[128,128]{1,0:T(8,128)}, f32[128,128]{1,0:T(8,128)S(1)}, u32[]{:S(2)}) copy-start(f32[128,128]{1,0:T(8,128)S(1)} %copy.139) | copy-start | bytes 196612
  165.6 172.3 %reduce-scatter.2.cloned.1.call-start = ((), (), s32[]{:S(2)}) async-start(), calls=%async_computation.2 | async-start | bytes 8912896 | tf_op jit(solution)/shard_map/reduce_scatter | solution.py:198
  183.4 46.1 %copy-start.49 = (f32[128]{0:T(128)S(1)}, f32[128]{0:T(128)}, u32[]{:S(2)}) copy-start(f32[128]{0:T(128)} %copy-done.48) | copy-start | bytes 1540
  183.4 50.2 %copy-start.6 = (f32[128,1,128]{2,0,1:T(8,128)S(1)}, f32[128,1,128]{2,0,1:T(8,128)}, u32[]{:S(2)}) copy-start(f32[128,1,128]{2,0,1:T(8,128)} %convolution_bitcast_fusion.13) | copy-start | bytes 196612
  183.4 50.2 %copy-start.7 = (f32[128,1,128]{2,0,1:T(8,128)S(1)}, f32[128,1,128]{2,0,1:T(8,128)}, u32[]{:S(2)}) copy-start(f32[128,1,128]{2,0,1:T(8,128)} %convolution_bitcast_fusion.12) | copy-start | bytes 196612
  183.5 50.2 %copy-start.8 = (f32[128,1,128]{2,0,1:T(8,128)S(1)}, f32[128,1,128]{2,0,1:T(8,128)}, u32[]{:S(2)}) copy-start(f32[128,1,128]{2,0,1:T(8,128)} %fusion.10) | copy-start | bytes 196612
  183.5 50.2 %copy-start.9 = (f32[128,1,128]{2,0,1:T(8,128)S(1)}, f32[128,1,128]{2,0,1:T(8,128)}, u32[]{:S(2)}) copy-start(f32[128,1,128]{2,0,1:T(8,128)} %fusion.9) | copy-start | bytes 196612
  (45 other events, 467.3 us)
Sparse Core Ops, SparseCore 0:
  13.0 46.1 all-gather.5
  81.4 55.2 all-gather.9
  165.7 53.1 all-gather.7
  245.5 92.3 reduce-scatter.1
where the time goes:
time: 350 us; the launch traced here: 346 us
  waiting for transfers between devices  166 us (47%)
  matrix products  55.3 us (16%)
  other arithmetic  42.2 us (12%)
  blocking collectives  38.8 us (11%)
  local copies, waits for them, and re-layouts  28.1 us (8%)
  between operations  14.9 us (4%)
    reduce_scatter x1, waiting for transfers between devices, per_device(): lax.psum_scatter(term + jnp.dot(dt_grad, w_dt, preferred_element_type=jnp...  88.3 us
    all_gather x2, waiting for transfers between devices, entering(): gathered = jax.tree.map(lambda a: lax.all_gather(a, axis), part)  71.8 us
    all_gather x1, blocking collectives, per_device(): lax.all_gather(scale_power, 'tensor', axis=0, tiled=True)  21.7 us
    all_gather x1, blocking collectives, entering(): gathered = jax.tree.map(lambda a: lax.all_gather(a, axis), part)  17.1 us
    add x15, other arithmetic, chain_combine(): later[0][:, :, None, None] * earlier[1] + later[1]  15.9 us
    mul x2, local copies, waits for them, and re-layouts, dequantize(): restored = blocks_view * scale_power.astype(jnp.float32)[:, :, None]  13 us
    dot_general x1, matrix products, per_device(): jnp.dot(quantized, w_proj, preferred_element_type=jnp.float32)  10.2 us
    dot_general x6, matrix products, block_parts(): jnp.einsum('tsge,sgep->tgep', mixing, x_heads, precision=PRECISE)  9.51 us
  transfers between devices with their start and end apart: 4, of which 4 were waited for; matrix products, arithmetic and copies ran while one was open for 12% of the time, Pallas kernels for 0%

commit v1 on v0

v1 whole, which is shorter than its diff:
```python
import jax
import jax.numpy as jnp
from jax import lax
from jax.experimental import pallas as pl
from jax.experimental.pallas import tpu as pltpu
from jax.sharding import PartitionSpec as P

BF = jnp.bfloat16
F32 = jnp.float32
MESH = pl.DeviceIdType.MESH

PLANES = 8
SPANS = 16
ROWS = 16
SPAN = 256
FEAT = 8192
HEADS = 8
HDIM = 64
XW = HEADS * HDIM
STATE = 128
PROJ = XW + 2 * STATE
PIECES = 4
PIECE = FEAT // PIECES
HALF = PIECES // 2
PART = XW // SPANS
SLOT = {0: 0, 1: 1, 7: 2, 2: 3, 6: 4, 3: 5, 5: 6, 4: 7}
NEAR = 5 * 32

NN = (((1,), (0,)), ((), ()))
NT = (((1,), (1,)), ((), ()))
TN = (((0,), (0,)), ((), ()))


def mm(a, b, dims=NN):
    return lax.dot_general(a, b, dims, preferred_element_type=F32)


def cols(piece):
    return pl.ds(piece * PIECE, PIECE)


def quantize(rows):
    lane = lax.broadcasted_iota(jnp.int32, rows.shape, 1)
    largest = jnp.abs(rows)
    for step in (1, 2, 4, 8, 16):
        below = pltpu.roll(largest, step, 1)
        above = pltpu.roll(largest, 128 - step, 1)
        largest = jnp.maximum(largest, jnp.where((lane & step) != 0, below, above))
    power = jnp.exp2(jnp.floor(jnp.log2(jnp.maximum(largest, 2.0**-39)))).astype(BF).astype(F32)
    power = jnp.where(power > largest, power * 0.5, power)
    power = jnp.where(power * 2.0 <= largest, power * 2.0, power)
    scale = jnp.where(largest >= 2.0**-39, power * 2.0**-8, 2.0**-48)
    lifted = rows * 2.0**20
    normal = (rows + lifted) - lifted
    anchor = scale * (1.5 * 2.0**14)
    small = (rows + anchor) - anchor
    snapped = jnp.where(jnp.abs(rows) < scale * 2.0**-6, small, normal)
    bound = scale * 448.0
    return jnp.clip(snapped, -bound, bound)


def split3(values):
    first = values.astype(BF)
    rest = values - first.astype(F32)
    second = rest.astype(BF)
    third = (rest - second.astype(F32)).astype(BF)
    return first, second, third


def sums(values, chosen):
    first, second, third = split3(values)
    stacked = jnp.concatenate(
        [first.astype(F32), second.astype(F32), third.astype(F32), jnp.zeros_like(values)], axis=0
    ).astype(BF)
    out = mm(stacked, chosen)
    return out[0:8] + out[8:16] + out[16:24]


def column(scalars):
    row = lax.broadcasted_iota(jnp.int32, (HEADS, SPAN), 0)
    out = jnp.zeros((HEADS, SPAN), F32)
    for head in range(HEADS):
        out = jnp.where(row == head, scalars[head], out)
    return out


def head_rows(head):
    return pl.ds(head * HDIM, HDIM)


def kernel(
    hid, w_hbm, wdt_ref, bias_ref, alog_ref, skip_ref, docs, go,
    y_out, gh_out,
    w, wdt, xb, acc, dacc, bias_m, gyt, pn, dn_, ptx, dst, ut, gyw, kut, yt, dut, ds_,
    xs, xr, os_, or_, pg, dg, pga, dga, own, sbs, sbr, ru_s, ru_r, rd_s, rd_r,
    wsem, au_s, au_r, ad_s, ad_r, ab_s, ab_r, x1s, x1r, x2s, x2r,
    bu_s, bu_r, bd_s, bd_r, bb_s, bb_r,
):
    me = lax.axis_index("tensor")
    span = lax.axis_index("context")
    z = me // 2
    core = me % 2
    up = lax.rem(z + 1, PLANES) * 2 + core
    down = lax.rem(z + PLANES - 1, PLANES) * 2 + core
    twin = z * 2 + (1 - core)

    w_copy = pltpu.make_async_copy(w_hbm, w, wsem)
    w_copy.start()

    barrier = pltpu.get_barrier_semaphore()
    for near in (up, down, twin):
        pl.semaphore_signal(barrier, inc=1, device_id={"tensor": near}, device_id_type=MESH)

    def greet(step, carry):
        pl.semaphore_signal(
            barrier, inc=1, device_id={"context": lax.rem(span + step, SPANS)}, device_id_type=MESH
        )
        return carry

    lax.fori_loop(1, SPANS, greet, 0)

    def block(place, half, piece):
        return xb.at[pl.ds(SLOT[place % PLANES] * 32 + half * 16, ROWS), cols(piece)]

    def to_up(step, piece):
        return pltpu.make_async_remote_copy(
            src_ref=block(-step, 0, piece), dst_ref=block(-step - 1, 0, piece),
            send_sem=au_s.at[step, piece], recv_sem=au_r.at[step, piece],
            device_id={"tensor": up}, device_id_type=MESH,
        )

    def to_down(step, piece):
        return pltpu.make_async_remote_copy(
            src_ref=block(step, 0, piece), dst_ref=block(step + 1, 0, piece),
            send_sem=ad_s.at[step, piece], recv_sem=ad_r.at[step, piece],
            device_id={"tensor": down}, device_id_type=MESH,
        )

    def to_twin(place, piece):
        place = place % PLANES
        return pltpu.make_async_remote_copy(
            src_ref=block(place, 0, piece), dst_ref=block(place, 1, piece),
            send_sem=ab_s.at[place, piece], recv_sem=ab_r.at[place, piece],
            device_id={"tensor": twin}, device_id_type=MESH,
        )

    tiles = PIECE // 128
    for piece in range(PIECES):
        part = hid[:, piece * PIECE : (piece + 1) * PIECE].astype(F32)
        stacked = jnp.concatenate(
            [part[:, i * 128 : (i + 1) * 128] for i in range(tiles)], axis=0
        )
        snapped = quantize(stacked)
        flat = jnp.concatenate(
            [snapped[i * ROWS : (i + 1) * ROWS] for i in range(tiles)], axis=1
        )
        xb[0:ROWS, piece * PIECE : (piece + 1) * PIECE] = flat.astype(BF)
        if piece == 0:
            pl.semaphore_wait(barrier, SPANS - 1 + 3)
        to_up(0, piece).start()
        to_down(0, piece).start()
        to_twin(0, piece).start()

    wdt[0:16, :] = jnp.concatenate(
        [wdt_ref[...].astype(F32), jnp.zeros((8, FEAT), F32)], axis=0
    ).astype(BF)
    wdt[16:128, :] = jnp.zeros((112, FEAT), BF)
    first_token = span * SPAN

    def segment(positions):
        out = jnp.full(positions.shape, -1, jnp.int32)
        begin = jnp.int32(0)
        for doc in range(8):
            out = out + jnp.where(positions >= begin, 1, 0)
            begin = begin + docs[doc]
        return out

    row_pos = first_token + lax.broadcasted_iota(jnp.int32, (SPAN, SPAN), 0)
    col_pos = first_token + lax.broadcasted_iota(jnp.int32, (SPAN, SPAN), 1)
    bias_m[...] = jnp.where(
        (row_pos >= col_pos) & (segment(row_pos) == segment(col_pos)), 0.0, -1e30
    )
    token = first_token + lax.broadcasted_iota(jnp.int32, (HEADS, SPAN), 1)
    seg = segment(token)
    seg_before = segment(jnp.zeros((HEADS, SPAN), jnp.int32) + (first_token - 1))
    seg_last = segment(jnp.zeros((HEADS, SPAN), jnp.int32) + (first_token + SPAN - 1))
    continues = jnp.where(seg == seg_before, 1.0, 0.0)
    in_last = jnp.where(seg == seg_last, 1.0, 0.0)
    through = jnp.where(seg_last == seg_before, 1.0, 0.0)
    gyt[...] = jnp.transpose(go[...].astype(F32)).astype(BF)

    def project(first, last):
        for piece in range(PIECES):
            rows = xb[first:last, piece * PIECE : (piece + 1) * PIECE]
            part = mm(rows, w[piece * PIECE : (piece + 1) * PIECE, :])
            dpart = mm(rows, wdt[:, piece * PIECE : (piece + 1) * PIECE], NT)
            if piece == 0:
                acc[first:last, :] = part
                dacc[first:last, :] = dpart
            else:
                acc[first:last, :] += part
                dacc[first:last, :] += dpart

    for step in range(3):
        for piece in range(PIECES):
            to_up(step, piece).wait_recv()
            if step < 2 or piece < HALF:
                to_up(step + 1, piece).start()
            to_twin(-step - 1, piece).start()
            to_down(step, piece).wait_recv()
            if step < 2 or piece >= HALF:
                to_down(step + 1, piece).start()
            to_twin(step + 1, piece).start()
        if step == 1:
            w_copy.wait()
            for place in (0, 1, 7, 2, 6):
                for piece in range(PIECES):
                    to_twin(place, piece).wait_recv()
            project(0, NEAR)
    for piece in range(HALF):
        to_up(3, piece).wait_recv()
        to_twin(4, piece).start()
        to_down(3, piece + HALF).wait_recv()
        to_twin(4, piece + HALF).start()
    for place in (3, 5, 4):
        for piece in range(PIECES):
            to_twin(place, piece).wait_recv()
    project(NEAR, SPAN)
    for piece in range(PIECES):
        for step in range(4):
            if step < 3 or piece < HALF:
                to_up(step, piece).wait_send()
            if step < 3 or piece >= HALF:
                to_down(step, piece).wait_send()
        for place in range(PLANES):
            to_twin(place, piece).wait_send()

    def home(place, half):
        owner = lax.rem(z + place, PLANES) * 2 + (core if half == 0 else 1 - core)
        return pl.ds(pl.multiple_of(owner * ROWS, ROWS), ROWS)

    for place in range(PLANES):
        for half in range(2):
            at = SLOT[place] * 32 + half * 16
            pn[home(place, half), :] = acc[at : at + 16, :].astype(BF).astype(F32)
            dn_[home(place, half), :] = dacc[at : at + 16, :]

    natural = pn[:, XW:PROJ]
    natural = (natural / (1.0 + jnp.exp(-natural))).astype(BF)
    b_nat = natural[:, 0:STATE]
    c_nat = natural[:, STATE : 2 * STATE]
    pt = jnp.transpose(pn[...])
    gate = 1.0 / (1.0 + jnp.exp(-pt))
    ptx[...] = pt * gate
    dst[...] = gate * (1.0 + pt * (1.0 - gate))
    b_t = ptx[XW : XW + STATE, :].astype(BF)
    c_t = ptx[XW + STATE : PROJ, :].astype(BF)

    dt_arg = jnp.transpose(dn_[...])[0:HEADS, :] + column(bias_ref)
    dt = jnp.maximum(dt_arg, 0.0) + jnp.log1p(jnp.exp(-jnp.abs(dt_arg)))
    dt_gate = 1.0 / (1.0 + jnp.exp(-dt_arg))
    rate = -jnp.exp(column(alog_ref))
    skip = column(skip_ref)
    line = lax.broadcasted_iota(jnp.int32, (SPAN, SPAN), 0)
    lane = lax.broadcasted_iota(jnp.int32, (SPAN, SPAN), 1)
    upto = jnp.where(line <= lane, 1.0, 0.0).astype(BF)
    since = jnp.where(line >= lane, 1.0, 0.0).astype(BF)
    before = jnp.where(line < lane, 1.0, 0.0).astype(BF)
    cum = sums(dt * rate, upto)
    cum_col = jnp.transpose(jnp.concatenate([cum, jnp.zeros((120, SPAN), F32)], axis=0))
    cum_last = jnp.broadcast_to(cum[:, SPAN - 1 : SPAN], (HEADS, SPAN))
    carry_w = jnp.exp(cum) * continues
    keep_w = jnp.exp(cum_last - cum) * in_last
    total = jnp.exp(cum_last) * through

    for head in range(HEADS):
        at = head_rows(head)
        u = ptx[at, :] * dt[head : head + 1, :]
        ut[at, :] = u.astype(BF)
        kut[at, :] = (u * keep_w[head : head + 1, :]).astype(BF)
        gyw[at, :] = (gyt[at, :].astype(F32) * carry_w[head : head + 1, :]).astype(BF)
    end_state = mm(kut[...], b_nat).astype(BF)
    from_out = mm(gyw[...], c_nat).astype(BF)
    note_row = lax.broadcasted_iota(jnp.int32, (16, 128), 0)
    for part in range(SPANS):
        at = slice(part * PART, (part + 1) * PART)
        xs[part, 0:PART, :] = end_state[at]
        xs[part, PART : 2 * PART, :] = from_out[at]
        head = part * PART // HDIM
        decay = total[head : head + 1, 0:128]
        high = decay.astype(BF).astype(F32)
        xs[part, 2 * PART : 2 * PART + 16, :] = jnp.where(
            note_row == 0, high, jnp.where(note_row == 1, decay - high, 0.0)
        ).astype(BF)

    def other(step):
        return lax.rem(span + step, SPANS)

    def out1(step):
        return pltpu.make_async_remote_copy(
            src_ref=xs.at[other(step)], dst_ref=xr.at[span],
            send_sem=x1s.at[other(step)], recv_sem=x1r.at[span],
            device_id={"context": other(step)}, device_id_type=MESH,
        )

    def in1(step):
        return pltpu.make_async_remote_copy(
            src_ref=xs.at[other(step)], dst_ref=xr.at[other(step)],
            send_sem=x1s.at[other(step)], recv_sem=x1r.at[other(step)],
            device_id={"context": other(step)}, device_id_type=MESH,
        )

    def out2(step):
        return pltpu.make_async_remote_copy(
            src_ref=os_.at[other(step)], dst_ref=or_.at[span],
            send_sem=x2s.at[other(step)], recv_sem=x2r.at[span],
            device_id={"context": other(step)}, device_id_type=MESH,
        )

    def in2(step):
        return pltpu.make_async_remote_copy(
            src_ref=os_.at[other(step)], dst_ref=or_.at[other(step)],
            send_sem=x2s.at[other(step)], recv_sem=x2r.at[other(step)],
            device_id={"context": other(step)}, device_id_type=MESH,
        )

    def every(action):
        def one(step, carry):
            action(step)
            return carry

        lax.fori_loop(1, SPANS, one, 0)

    every(lambda step: out1(step).start())
    xr[span] = xs[span]

    scores = mm(c_nat, b_t)
    low = jnp.where(lax.broadcasted_iota(jnp.int32, (1, 128), 1) < HDIM, 1.0, 0.0).astype(BF)
    high_half = jnp.where(lax.broadcasted_iota(jnp.int32, (1, 128), 1) < HDIM, 0.0, 1.0).astype(BF)

    def inner(head):
        at = head_rows(head)
        pair = head // 2 * 128
        gap = cum_col[:, head : head + 1] - cum[head : head + 1, :] + bias_m[...]
        decay = jnp.exp(gap)
        mixing = (scores * decay).astype(BF)
        yt[at, :] = mm(ut[at, :], mixing, NT)
        dut[at, :] = mm(gyt[at, :], mixing)
        picked = go[:, pair : pair + 128] * (low if head % 2 == 0 else high_half)
        products = mm(picked, ut[pair : pair + 128, :])
        if head == 0:
            ds_[...] = products * decay
        else:
            ds_[...] += products * decay

    for head in range(HEADS // 2):
        inner(head)

    every(lambda step: in1(step).wait_recv())
    running = jnp.zeros((PART, STATE), F32)
    for source in range(SPANS):
        os_[source, 0:PART, :] = running.astype(BF)
        note = xr[source, 2 * PART : 2 * PART + 16, :].astype(F32)
        decay = note[0:1] + note[1:2]
        running = decay * running + xr[source, 0:PART, :].astype(F32)
    running = jnp.zeros((PART, STATE), F32)
    for source in reversed(range(SPANS)):
        os_[source, PART : 2 * PART, :] = running.astype(BF)
        note = xr[source, 2 * PART : 2 * PART + 16, :].astype(F32)
        decay = note[0:1] + note[1:2]
        running = decay * running + xr[source, PART : 2 * PART, :].astype(F32)
    every(lambda step: out2(step).start())
    or_[span] = os_[span]

    for head in range(HEADS // 2, HEADS):
        inner(head)
    ds = ds_[...].astype(BF)
    dc_t = mm(b_t, ds, NT)
    db_t = mm(c_t, ds)

    every(lambda step: in2(step).wait_recv())
    state_in = or_[:, 0:PART, :].reshape(XW, STATE)
    state_grad = or_[:, PART : 2 * PART, :].reshape(XW, STATE)
    carried = mm(state_in, c_t)
    reach = mm(state_grad, b_t)
    dc_t = dc_t + mm(state_in, gyw[...], TN)
    db_t = db_t + mm(state_grad, kut[...], TN)

    from_rows, from_u, from_keep, direct, ends = [], [], [], [], []
    for head in range(HEADS):
        at = head_rows(head)
        rows = slice(head * HDIM, (head + 1) * HDIM)
        x = ptx[at, :]
        gy = gyt[at, :].astype(F32)
        u = ut[at, :].astype(F32)
        y = yt[at, :] + carried[rows] * carry_w[head : head + 1, :]
        late = reach[rows] * keep_w[head : head + 1, :]
        du_here = dut[at, :]
        du = du_here + late
        from_rows.append(jnp.sum(gy * y, axis=0, keepdims=True))
        from_u.append(jnp.sum(u * du_here, axis=0, keepdims=True))
        from_keep.append(jnp.sum(u * late, axis=0, keepdims=True))
        direct.append(jnp.sum(x * du, axis=0, keepdims=True))
        ends.append(
            jnp.sum(state_in[rows].astype(F32) * state_grad[rows].astype(F32), axis=0, keepdims=True)
        )
        dx = du * dt[head : head + 1, :] + gy * skip[head : head + 1, :]
        pg[at, :] = dx * dst[at, :]
        yt[at, :] = y + x * skip[head : head + 1, :]
    pg[XW : XW + STATE, :] = db_t * dst[XW : XW + STATE, :]
    pg[XW + STATE : PROJ, :] = dc_t * dst[XW + STATE : PROJ, :]
    gap_grad = jnp.concatenate(from_rows, axis=0) - jnp.concatenate(from_u, axis=0)
    end_grad = jnp.sum(jnp.concatenate(ends, axis=0), axis=1, keepdims=True)
    log_grad = (
        sums(gap_grad, since)
        + sums(jnp.concatenate(from_keep, axis=0), before)
        + total * end_grad
    )
    dt_grad = (jnp.concatenate(direct, axis=0) + rate * log_grad) * dt_gate

    pn[...] = jnp.transpose(pg[...])
    dn_[...] = jnp.transpose(jnp.concatenate([dt_grad, jnp.zeros((120, SPAN), F32)], axis=0))
    for place in range(PLANES):
        for half in range(2):
            at = half * 128 + SLOT[place] * 16
            pga[at : at + 16, :] = pn[home(place, half), :].astype(BF)
            dga[at : at + 16, :] = dn_[home(place, half), :].astype(BF)

    def multiply(piece):
        width = 512

        def one(step, carry):
            at = pl.multiple_of(piece * PIECE + step * width, width)
            term = mm(pga[...], w[pl.ds(at, width), :], NT)
            term = term + mm(dga[...], wdt[:, pl.ds(at, width)])
            own[:, pl.ds(at, width)] = term[0:128]
            sbs[:, pl.ds(at, width)] = term[128:256].astype(BF)
            return carry

        lax.fori_loop(0, PIECE // width, one, 0)

    def swap(piece):
        return pltpu.make_async_remote_copy(
            src_ref=sbs.at[:, cols(piece)], dst_ref=sbr.at[:, cols(piece)],
            send_sem=bb_s.at[piece], recv_sem=bb_r.at[piece],
            device_id={"tensor": twin}, device_id_type=MESH,
        )

    def pass_up(step, piece):
        return pltpu.make_async_remote_copy(
            src_ref=ru_s.at[step, :, cols(piece)], dst_ref=ru_r.at[step, :, cols(piece)],
            send_sem=bu_s.at[step, piece], recv_sem=bu_r.at[step, piece],
            device_id={"tensor": up}, device_id_type=MESH,
        )

    def pass_down(step, piece):
        return pltpu.make_async_remote_copy(
            src_ref=rd_s.at[step, :, cols(piece)], dst_ref=rd_r.at[step, :, cols(piece)],
            send_sem=bd_s.at[step, piece], recv_sem=bd_r.at[step, piece],
            device_id={"tensor": down}, device_id_type=MESH,
        )

    def pair_sum(place, piece):
        at = slice(SLOT[place % PLANES] * 16, SLOT[place % PLANES] * 16 + 16)
        return own[at, cols(piece)] + sbr[at, cols(piece)].astype(F32)

    def go_up(step, piece):
        value = pair_sum(4 - step, piece)
        if step > 1 or (step == 1 and piece < HALF):
            pass_up(step - 1, piece).wait_recv()
            value = value + ru_r[step - 1, :, cols(piece)].astype(F32)
        ru_s[step, :, cols(piece)] = value.astype(BF)
        pass_up(step, piece).start()

    def go_down(step, piece):
        value = pair_sum(4 + step, piece)
        if step > 1 or (step == 1 and piece >= HALF):
            pass_down(step - 1, piece).wait_recv()
            value = value + rd_r[step - 1, :, cols(piece)].astype(F32)
        rd_s[step, :, cols(piece)] = value.astype(BF)
        pass_down(step, piece).start()

    order = (0, 2, 1, 3)
    for at, piece in enumerate(order):
        multiply(piece)
        swap(piece).start()
        if at > 0:
            ready = order[at - 1]
            swap(ready).wait_recv()
            (go_up if ready < HALF else go_down)(0, ready)
    ready = order[-1]
    swap(ready).wait_recv()
    (go_up if ready < HALF else go_down)(0, ready)
    for step in range(1, 4):
        for up_piece, down_piece in ((2, 0), (3, 1), (0, 2), (1, 3)):
            go_up(step, up_piece)
            go_down(step, down_piece)
        if step == 1:
            y_out[...] = jnp.transpose(yt[...]).astype(BF)
    for piece in (2, 0, 3, 1):
        pass_up(3, piece).wait_recv()
        pass_down(3, piece).wait_recv()
        value = pair_sum(0, piece)
        value = value + ru_r[3, :, cols(piece)].astype(F32) + rd_r[3, :, cols(piece)].astype(F32)
        gh_out[:, cols(piece)] = value.astype(BF)
    for piece in range(PIECES):
        swap(piece).wait_send()
        for step in range(4):
            if step > 0 or piece < HALF:
                pass_up(step, piece).wait_send()
            if step > 0 or piece >= HALF:
                pass_down(step, piece).wait_send()
    every(lambda step: out1(step).wait_send())
    every(lambda step: out2(step).wait_send())


def per_device(hidden, w_proj, w_dt, dt_bias, a_log, d_skip, doc_lengths, grad_out):
    vmem = pl.BlockSpec(memory_space=pltpu.VMEM)
    smem = pl.BlockSpec(memory_space=pltpu.SMEM)
    dma = pltpu.SemaphoreType.DMA
    return pl.pallas_call(
        kernel,
        out_shape=(
            jax.ShapeDtypeStruct((SPAN, XW), BF),
            jax.ShapeDtypeStruct((ROWS, FEAT), BF),
        ),
        in_specs=[vmem, pl.BlockSpec(memory_space=pl.ANY), vmem, smem, smem, smem, smem, vmem],
        out_specs=(vmem, vmem),
        scratch_shapes=[
            pltpu.VMEM((FEAT, PROJ), BF),
            pltpu.VMEM((128, FEAT), BF),
            pltpu.VMEM((SPAN, FEAT), BF),
            pltpu.VMEM((SPAN, PROJ), F32),
            pltpu.VMEM((SPAN, 128), F32),
            pltpu.VMEM((SPAN, SPAN), F32),
            pltpu.VMEM((XW, SPAN), BF),
            pltpu.VMEM((SPAN, PROJ), F32),
            pltpu.VMEM((SPAN, 128), F32),
            pltpu.VMEM((PROJ, SPAN), F32),
            pltpu.VMEM((PROJ, SPAN), F32),
            pltpu.VMEM((XW, SPAN), BF),
            pltpu.VMEM((XW, SPAN), BF),
            pltpu.VMEM((XW, SPAN), BF),
            pltpu.VMEM((XW, SPAN), F32),
            pltpu.VMEM((XW, SPAN), F32),
            pltpu.VMEM((SPAN, SPAN), F32),
            pltpu.VMEM((SPANS, 2 * PART + 16, STATE), BF),
            pltpu.VMEM((SPANS, 2 * PART + 16, STATE), BF),
            pltpu.VMEM((SPANS, 2 * PART, STATE), BF),
            pltpu.VMEM((SPANS, 2 * PART, STATE), BF),
            pltpu.VMEM((PROJ, SPAN), F32),
            pltpu.VMEM((128, SPAN), F32),
            pltpu.VMEM((SPAN, PROJ), BF),
            pltpu.VMEM((SPAN, 128), BF),
            pltpu.VMEM((128, FEAT), F32),
            pltpu.VMEM((128, FEAT), BF),
            pltpu.VMEM((128, FEAT), BF),
            pltpu.VMEM((4, ROWS, FEAT), BF),
            pltpu.VMEM((4, ROWS, FEAT), BF),
            pltpu.VMEM((4, ROWS, FEAT), BF),
            pltpu.VMEM((4, ROWS, FEAT), BF),
            dma,
            dma((4, PIECES)), dma((4, PIECES)), dma((4, PIECES)), dma((4, PIECES)),
            dma((PLANES, PIECES)), dma((PLANES, PIECES)),
            dma((SPANS,)), dma((SPANS,)), dma((SPANS,)), dma((SPANS,)),
            dma((4, PIECES)), dma((4, PIECES)), dma((4, PIECES)), dma((4, PIECES)),
            dma((PIECES,)), dma((PIECES,)),
        ],
        compiler_params=pltpu.CompilerParams(
            collective_id=0, has_side_effects=True, vmem_limit_bytes=60 * 1024 * 1024
        ),
        name="layer",
    )(hidden, w_proj, w_dt, dt_bias, a_log, d_skip, doc_lengths, grad_out)


def solution(mesh):
    placed = (
        P(("context", "tensor"), None),
        P(None, "tensor"),
        P("tensor", None),
        P("tensor"),
        P("tensor"),
        P("tensor"),
        P(),
        P("context", "tensor"),
    )
    return jax.shard_map(
        per_device,
        mesh=mesh,
        in_specs=placed,
        out_specs=(P("context", "tensor"), P(("context", "tensor"), None)),
        check_vma=False,
    )
```

time: 350 us -> 90 us (0.26); the launches traced: 346 us -> 89.8 us
  waiting for transfers between devices: 166 us -> 0 us
  Pallas kernels: 0 us -> 85.9 us
  matrix products: 55.3 us -> 0 us
  other arithmetic: 42.2 us -> 0 us
  blocking collectives: 38.8 us -> 0 us
  local copies, waits for them, and re-layouts: 28.1 us -> 3.34 us
  between operations: 14.9 us -> 0.64 us
    reduce_scatter x1 -> x0, waiting for transfers between devices: 88.3 us -> none  [per_device(): lax.psum_scatter(term + jnp.dot(dt_grad, w_dt, preferred_element_type=jnp...]
    pallas_call x0 -> x1, Pallas kernels: none -> 85.9 us  [per_device(): pl.pallas_call(kernel, out_shape=(jax.ShapeDtypeStruct((SPAN, XW), BF), j...]
    all_gather x3 -> x0, waiting for transfers between devices: 77.3 us -> none  [the longest x2 71.8 us: entering(): gathered = jax.tree.map(lambda a: lax.all_gather(a, axis), part)]
    dot_general x28 -> x0, matrix products: 55.3 us -> none  [the longest x1 10.2 us: per_device(): jnp.dot(quantized, w_proj, preferred_element_type=jnp.float32)]
    all_gather x2 -> x0, blocking collectives: 38.8 us -> none  [the longest x1 21.7 us: per_device(): lax.all_gather(scale_power, 'tensor', axis=0, tiled=True)]
    add x18 -> x0, other arithmetic: 16.1 us -> none  [the longest x15 15.9 us: chain_combine(): later[0][:, :, None, None] * earlier[1] + later[1]]
    mul x22 -> x0, local copies, waits for them, and re-layouts: 13.6 us -> none  [the longest x2 13 us: dequantize(): restored = blocks_view * scale_power.astype(jnp.float32)[:, :, None]]
    convert_element_type x4 -> x0, other arithmetic: 5.88 us -> none  [the longest x1 2.46 us: block_parts(): in_last = (segments == segments[-1]).astype(jnp.float32)]
  transfers between devices with their start and end apart: 4 -> 0, of which waited for: 4 -> 0; matrix products, arithmetic and copies ran while one was open for 12% -> 0% of each run, Pallas kernels for 0% -> 0%
where the time goes in v1:
time: 90 us; the launch traced here: 89.8 us
  Pallas kernels  85.9 us (95%)
  local copies, waits for them, and re-layouts  3.34 us (4%)
    pallas_call x1, Pallas kernels, per_device(): pl.pallas_call(kernel, out_shape=(jax.ShapeDtypeStruct((SPAN, XW), BF), j...  85.9 us
    unnamed x2, local copies, waits for them, and re-layouts  3.34 us

profile of v1, /device:TPU:1, one launch (start us, length us, event | category | flops | bytes accessed | tf_op | source)
XLA Modules:
  0.0 89.8 jit_solution(9383375581085731107)
XLA Ops:
  0.6 85.9 %layer.1 = (bf16[256,512]{1,0:T(8,128)(2,1)}, bf16[16,8192]{1,0:T(8,128)(2,1)}) custom-call(bf16[16,8192]{1,0:T(8,128)(2,1)} %hid.1, bf16[8192,768]{1,0:T(8,128)(2,1)} %w_hbm.1, bf16[8,8192]{1,0:T(8,128)(2,1)} %wdt_ref.1, f32[8]{0:T(128)} %bias_ref.1, f32[8]{0:T(128)} %alog_ref.1, f32[8]{0:T(128)} %skip_ref.1, s32[8]{0:T(128)} %docs.1, bf16[256,512]{1,0:T(8,128)(2,1)} %go.1), custom_call_target="tpu_custom_call" | custom-call | tf_op jit(solution)/shard_map/layer/pallas_call | solution.py:521
  86.5 1.7 %copy.12 = bf16[256,512]{1,0:T(8,128)(2,1)} copy(bf16[256,512]{1,0:T(8,128)(2,1)} %get-tuple-element.4) | data formatting | bytes 524288
  88.2 1.7 %copy.13 = bf16[16,8192]{1,0:T(8,128)(2,1)} copy(bf16[16,8192]{1,0:T(8,128)(2,1)} %get-tuple-element.5) | data formatting | bytes 524288

commit v2 on v1

--- a/solution.py
+++ b/solution.py
@@ -19,9 +19,8 @@
 XW = HEADS * HDIM
 STATE = 128
 PROJ = XW + 2 * STATE
-PIECES = 4
-PIECE = FEAT // PIECES
-HALF = PIECES // 2
+WIDE = PROJ + 128
+QUARTER = FEAT // 4
 PART = XW // SPANS
 SLOT = {0: 0, 1: 1, 7: 2, 2: 3, 6: 4, 3: 5, 5: 6, 4: 7}
 NEAR = 5 * 32
@@ -35,8 +34,8 @@
     return lax.dot_general(a, b, dims, preferred_element_type=F32)
 
 
-def cols(piece):
-    return pl.ds(piece * PIECE, PIECE)
+def cols(quarter, count=1):
+    return pl.ds(quarter * QUARTER, count * QUARTER)
 
 
 def quantize(rows):
@@ -91,10 +90,10 @@
 def kernel(
     hid, w_hbm, wdt_ref, bias_ref, alog_ref, skip_ref, docs, go,
     y_out, gh_out,
-    w, wdt, xb, acc, dacc, bias_m, gyt, pn, dn_, ptx, dst, ut, gyw, kut, yt, dut, ds_,
-    xs, xr, os_, or_, pg, dg, pga, dga, own, sbs, sbr, ru_s, ru_r, rd_s, rd_r,
+    w, xb, acc, bias_m, gyt, pn, ptx, dst, ut, gyw, kut, yt, dut, ds_,
+    xs, xr, os_, or_, pg, pga, own, sbs, sbr, ru_s, ru_r, rd_s, rd_r,
     wsem, au_s, au_r, ad_s, ad_r, ab_s, ab_r, x1s, x1r, x2s, x2r,
-    bu_s, bu_r, bd_s, bd_r, bb_s, bb_r,
+    bu_s, bu_r, bd_s, bd_r, bb_s, bb_r, bf_s, bf_r,
 ):
     me = lax.axis_index("tensor")
     span = lax.axis_index("context")
@@ -104,7 +103,7 @@
     down = lax.rem(z + PLANES - 1, PLANES) * 2 + core
     twin = z * 2 + (1 - core)
 
-    w_copy = pltpu.make_async_copy(w_hbm, w, wsem)
+    w_copy = pltpu.make_async_copy(w_hbm, w.at[:, 0:PROJ], wsem)
     w_copy.start()
 
     barrier = pltpu.get_barrier_semaphore()
@@ -119,34 +118,41 @@
 
     lax.fori_loop(1, SPANS, greet, 0)
 
-    def block(place, half, piece):
-        return xb.at[pl.ds(SLOT[place % PLANES] * 32 + half * 16, ROWS), cols(piece)]
-
-    def to_up(step, piece):
-        return pltpu.make_async_remote_copy(
-            src_ref=block(-step, 0, piece), dst_ref=block(-step - 1, 0, piece),
-            send_sem=au_s.at[step, piece], recv_sem=au_r.at[step, piece],
+    def block(place, half, quarter, count):
+        return xb.at[pl.ds(SLOT[place % PLANES] * 32 + half * 16, ROWS), cols(quarter, count)]
+
+    def to_up(step, quarter, count):
+        return pltpu.make_async_remote_copy(
+            src_ref=block(-step, 0, quarter, count), dst_ref=block(-step - 1, 0, quarter, count),
+            send_sem=au_s.at[step, quarter], recv_sem=au_r.at[step, quarter],
             device_id={"tensor": up}, device_id_type=MESH,
         )
 
-    def to_down(step, piece):
-        return pltpu.make_async_remote_copy(
-            src_ref=block(step, 0, piece), dst_ref=block(step + 1, 0, piece),
-            send_sem=ad_s.at[step, piece], recv_sem=ad_r.at[step, piece],
+    def to_down(step, quarter, count):
+        return pltpu.make_async_remote_copy(
+            src_ref=block(step, 0, quarter, count), dst_ref=block(step + 1, 0, quarter, count),
+            send_sem=ad_s.at[step, quarter], recv_sem=ad_r.at[step, quarter],
             device_id={"tensor": down}, device_id_type=MESH,
         )
 
-    def to_twin(place, piece):
+    def to_twin(place, quarter, count):
         place = place % PLANES
         return pltpu.make_async_remote_copy(
-            src_ref=block(place, 0, piece), dst_ref=block(place, 1, piece),
-            send_sem=ab_s.at[place, piece], recv_sem=ab_r.at[place, piece],
+            src_ref=block(place, 0, quarter, count), dst_ref=block(place, 1, quarter, count),
+            send_sem=ab_s.at[place, quarter], recv_sem=ab_r.at[place, quarter],
             device_id={"tensor": twin}, device_id_type=MESH,
         )
 
-    tiles = PIECE // 128
-    for piece in range(PIECES):
-        part = hid[:, piece * PIECE : (piece + 1) * PIECE].astype(F32)
+    quarters = ((0, 1), (1, 1), (2, 1), (3, 1))
+    halves = ((0, 2), (2, 2))
+    up_units = (quarters, halves, halves, quarters[:2])
+    down_units = (quarters[2:] + quarters[:2], halves[::-1], halves[::-1], quarters[2:])
+    twin_units = {0: ((0, 4),), 4: quarters}
+
+    tiles = QUARTER // 128
+
+    def encode(quarter):
+        part = hid[:, quarter * QUARTER : (quarter + 1) * QUARTER].astype(F32)
         stacked = jnp.concatenate(
             [part[:, i * 128 : (i + 1) * 128] for i in range(tiles)], axis=0
         )
@@ -154,17 +160,23 @@
         flat = jnp.concatenate(
             [snapped[i * ROWS : (i + 1) * ROWS] for i in range(tiles)], axis=1
         )
-        xb[0:ROWS, piece * PIECE : (piece + 1) * PIECE] = flat.astype(BF)
-        if piece == 0:
-            pl.semaphore_wait(barrier, SPANS - 1 + 3)
-        to_up(0, piece).start()
-        to_down(0, piece).start()
-        to_twin(0, piece).start()
-
-    wdt[0:16, :] = jnp.concatenate(
-        [wdt_ref[...].astype(F32), jnp.zeros((8, FEAT), F32)], axis=0
-    ).astype(BF)
-    wdt[16:128, :] = jnp.zeros((112, FEAT), BF)
+        xb[0:ROWS, quarter * QUARTER : (quarter + 1) * QUARTER] = flat.astype(BF)
+
+    encode(0)
+    pl.semaphore_wait(barrier, SPANS - 1 + 3)
+    to_up(0, 0, 1).start()
+    encode(2)
+    to_down(0, 2, 1).start()
+    encode(1)
+    to_up(0, 1, 1).start()
+    encode(3)
+    to_down(0, 3, 1).start()
+    to_up(0, 2, 1).start()
+    to_down(0, 0, 1).start()
+    to_up(0, 3, 1).start()
+    to_down(0, 1, 1).start()
+    to_twin(0, 0, 4).start()
+
     first_token = span * SPAN
 
     def segment(positions):
@@ -189,51 +201,59 @@
     through = jnp.where(seg_last == seg_before, 1.0, 0.0)
     gyt[...] = jnp.transpose(go[...].astype(F32)).astype(BF)
 
-    def project(first, last):
-        for piece in range(PIECES):
-            rows = xb[first:last, piece * PIECE : (piece + 1) * PIECE]
-            part = mm(rows, w[piece * PIECE : (piece + 1) * PIECE, :])
-            dpart = mm(rows, wdt[:, piece * PIECE : (piece + 1) * PIECE], NT)
-            if piece == 0:
-                acc[first:last, :] = part
-                dacc[first:last, :] = dpart
-            else:
-                acc[first:last, :] += part
-                dacc[first:last, :] += dpart
+    for quarter in range(4):
+        steps_w = wdt_ref[:, quarter * QUARTER : (quarter + 1) * QUARTER].astype(F32)
+        padded = jnp.concatenate([steps_w, jnp.zeros((120, QUARTER), F32)], axis=0)
+        w[cols(quarter), PROJ:WIDE] = jnp.transpose(padded).astype(BF)
+
+    def project(first, last, quarter, begin):
+        at = slice(quarter * QUARTER, (quarter + 1) * QUARTER)
+        part = mm(xb[first:last, at], w[at, :])
+        if begin:
+            acc[first:last, :] = part
+        else:
+            acc[first:last, :] += part
+
+    def arrived_twin(place):
+        for unit in twin_units.get(place, halves):
+            to_twin(place, *unit).wait_recv()
 
     for step in range(3):
-        for piece in range(PIECES):
-            to_up(step, piece).wait_recv()
-            if step < 2 or piece < HALF:
-                to_up(step + 1, piece).start()
-            to_twin(-step - 1, piece).start()
-            to_down(step, piece).wait_recv()
-            if step < 2 or piece >= HALF:
-                to_down(step + 1, piece).start()
-            to_twin(step + 1, piece).start()
+        for turn in range(2):
+            unit = halves[turn]
+            for got in quarters[2 * turn : 2 * turn + 2] if step == 0 else (unit,):
+                to_up(step, *got).wait_recv()
+            if step < 2:
+                to_up(step + 1, *unit).start()
+            elif turn == 0:
+                for part in up_units[3]:
+                    to_up(3, *part).start()
+            to_twin(-step - 1, *unit).start()
+            unit = halves[1 - turn]
+            for got in quarters[2 - 2 * turn : 4 - 2 * turn] if step == 0 else (unit,):
+                to_down(step, *got).wait_recv()
+            if step < 2:
+                to_down(step + 1, *unit).start()
+            elif turn == 0:
+                for part in down_units[3]:
+                    to_down(3, *part).start()
+            to_twin(step + 1, *unit).start()
         if step == 1:
             w_copy.wait()
             for place in (0, 1, 7, 2, 6):
-                for piece in range(PIECES):
-                    to_twin(place, piece).wait_recv()
-            project(0, NEAR)
-    for piece in range(HALF):
-        to_up(3, piece).wait_recv()
-        to_twin(4, piece).start()
-        to_down(3, piece + HALF).wait_recv()
-        to_twin(4, piece + HALF).start()
-    for place in (3, 5, 4):
-        for piece in range(PIECES):
-            to_twin(place, piece).wait_recv()
-    project(NEAR, SPAN)
-    for piece in range(PIECES):
-        for step in range(4):
-            if step < 3 or piece < HALF:
-                to_up(step, piece).wait_send()
-            if step < 3 or piece >= HALF:
-                to_down(step, piece).wait_send()
-        for place in range(PLANES):
-            to_twin(place, piece).wait_send()
+                arrived_twin(place)
+            for quarter in range(4):
+                project(0, NEAR, quarter, quarter == 0)
+    for at in range(2):
+        to_up(3, *up_units[3][at]).wait_recv()
+        to_twin(4, *up_units[3][at]).start()
+        to_down(3, *down_units[3][at]).wait_recv()
+        to_twin(4, *down_units[3][at]).start()
+    arrived_twin(3)
+    arrived_twin(5)
+    for quarter in (0, 2, 1, 3):
+        to_twin(4, quarter, 1).wait_recv()
+        project(NEAR, SPAN, quarter, quarter == 0)
 
     def home(place, half):
         owner = lax.rem(z + place, PLANES) * 2 + (core if half == 0 else 1 - core)
@@ -242,21 +262,22 @@
     for place in range(PLANES):
         for half in range(2):
             at = SLOT[place] * 32 + half * 16
-            pn[home(place, half), :] = acc[at : at + 16, :].astype(BF).astype(F32)
-            dn_[home(place, half), :] = dacc[at : at + 16, :]
+            pn[home(place, half), 0:PROJ] = acc[at : at + 16, 0:PROJ].astype(BF).astype(F32)
+            pn[home(place, half), PROJ:WIDE] = acc[at : at + 16, PROJ:WIDE]
 
     natural = pn[:, XW:PROJ]
     natural = (natural / (1.0 + jnp.exp(-natural))).astype(BF)
     b_nat = natural[:, 0:STATE]
     c_nat = natural[:, STATE : 2 * STATE]
-    pt = jnp.transpose(pn[...])
+    all_t = jnp.transpose(pn[...])
+    pt = all_t[0:PROJ]
     gate = 1.0 / (1.0 + jnp.exp(-pt))
     ptx[...] = pt * gate
     dst[...] = gate * (1.0 + pt * (1.0 - gate))
     b_t = ptx[XW : XW + STATE, :].astype(BF)
     c_t = ptx[XW + STATE : PROJ, :].astype(BF)
 
-    dt_arg = jnp.transpose(dn_[...])[0:HEADS, :] + column(bias_ref)
+    dt_arg = all_t[PROJ : PROJ + HEADS] + column(bias_ref)
     dt = jnp.maximum(dt_arg, 0.0) + jnp.log1p(jnp.exp(-jnp.abs(dt_arg)))
     dt_gate = 1.0 / (1.0 + jnp.exp(-dt_arg))
     rate = -jnp.exp(column(alog_ref))
@@ -418,98 +439,129 @@
     )
     dt_grad = (jnp.concatenate(direct, axis=0) + rate * log_grad) * dt_gate
 
+    pg[PROJ : PROJ + HEADS, :] = dt_grad
+    pg[PROJ + HEADS : WIDE, :] = jnp.zeros((128 - HEADS, SPAN), F32)
     pn[...] = jnp.transpose(pg[...])
-    dn_[...] = jnp.transpose(jnp.concatenate([dt_grad, jnp.zeros((120, SPAN), F32)], axis=0))
     for place in range(PLANES):
         for half in range(2):
             at = half * 128 + SLOT[place] * 16
             pga[at : at + 16, :] = pn[home(place, half), :].astype(BF)
-            dga[at : at + 16, :] = dn_[home(place, half), :].astype(BF)
-
-    def multiply(piece):
-        width = 512
-
-        def one(step, carry):
-            at = pl.multiple_of(piece * PIECE + step * width, width)
-            term = mm(pga[...], w[pl.ds(at, width), :], NT)
-            term = term + mm(dga[...], wdt[:, pl.ds(at, width)])
-            own[:, pl.ds(at, width)] = term[0:128]
-            sbs[:, pl.ds(at, width)] = term[128:256].astype(BF)
-            return carry
-
-        lax.fori_loop(0, PIECE // width, one, 0)
-
-    def swap(piece):
-        return pltpu.make_async_remote_copy(
-            src_ref=sbs.at[:, cols(piece)], dst_ref=sbr.at[:, cols(piece)],
-            send_sem=bb_s.at[piece], recv_sem=bb_r.at[piece],
+
+    def multiply(quarter):
+        term = mm(pga[...], w[quarter * QUARTER : (quarter + 1) * QUARTER, :], NT)
+        own[:, cols(quarter)] = term[0:128]
+        sbs[:, cols(quarter)] = term[128:256].astype(BF)
+
+    far = SLOT[4] * 16
+
+    def swap_far(quarter):
+        return pltpu.make_async_remote_copy(
+            src_ref=sbs.at[far : far + 16, cols(quarter)], dst_ref=sbr.at[far : far + 16, cols(quarter)],
+            send_sem=bf_s.at[quarter], recv_sem=bf_r.at[quarter],
             device_id={"tensor": twin}, device_id_type=MESH,
         )
 
-    def pass_up(step, piece):
-        return pltpu.make_async_remote_copy(
-            src_ref=ru_s.at[step, :, cols(piece)], dst_ref=ru_r.at[step, :, cols(piece)],
-            send_sem=bu_s.at[step, piece], recv_sem=bu_r.at[step, piece],
+    def swap(quarter):
+        return pltpu.make_async_remote_copy(
+            src_ref=sbs.at[0:far, cols(quarter)], dst_ref=sbr.at[0:far, cols(quarter)],
+            send_sem=bb_s.at[quarter], recv_sem=bb_r.at[quarter],
+            device_id={"tensor": twin}, device_id_type=MESH,
+        )
+
+    def pass_up(step, quarter, count):
+        return pltpu.make_async_remote_copy(
+            src_ref=ru_s.at[step, :, cols(quarter, count)], dst_ref=ru_r.at[step, :, cols(quarter, count)],
+            send_sem=bu_s.at[step, quarter], recv_sem=bu_r.at[step, quarter],
             device_id={"tensor": up}, device_id_type=MESH,
         )
 
-    def pass_down(step, piece):
-        return pltpu.make_async_remote_copy(
-            src_ref=rd_s.at[step, :, cols(piece)], dst_ref=rd_r.at[step, :, cols(piece)],
-            send_sem=bd_s.at[step, piece], recv_sem=bd_r.at[step, piece],
+    def pass_down(step, quarter, count):
+        return pltpu.make_async_remote_copy(
+            src_ref=rd_s.at[step, :, cols(quarter, count)], dst_ref=rd_r.at[step, :, cols(quarter, count)],
+            send_sem=bd_s.at[step, quarter], recv_sem=bd_r.at[step, quarter],
             device_id={"tensor": down}, device_id_type=MESH,
         )
 
-    def pair_sum(place, piece):
+    def pair_sum(place, quarter, count):
         at = slice(SLOT[place % PLANES] * 16, SLOT[place % PLANES] * 16 + 16)
-        return own[at, cols(piece)] + sbr[at, cols(piece)].astype(F32)
-
-    def go_up(step, piece):
-        value = pair_sum(4 - step, piece)
-        if step > 1 or (step == 1 and piece < HALF):
-            pass_up(step - 1, piece).wait_recv()
-            value = value + ru_r[step - 1, :, cols(piece)].astype(F32)
-        ru_s[step, :, cols(piece)] = value.astype(BF)
-        pass_up(step, piece).start()
-
-    def go_down(step, piece):
-        value = pair_sum(4 + step, piece)
-        if step > 1 or (step == 1 and piece >= HALF):
-            pass_down(step - 1, piece).wait_recv()
-            value = value + rd_r[step - 1, :, cols(piece)].astype(F32)
-        rd_s[step, :, cols(piece)] = value.astype(BF)
-        pass_down(step, piece).start()
-
-    order = (0, 2, 1, 3)
-    for at, piece in enumerate(order):
-        multiply(piece)
-        swap(piece).start()
-        if at > 0:
-            ready = order[at - 1]
-            swap(ready).wait_recv()
-            (go_up if ready < HALF else go_down)(0, ready)
-    ready = order[-1]
-    swap(ready).wait_recv()
-    (go_up if ready < HALF else go_down)(0, ready)
-    for step in range(1, 4):
-        for up_piece, down_piece in ((2, 0), (3, 1), (0, 2), (1, 3)):
-            go_up(step, up_piece)
-            go_down(step, down_piece)
-        if step == 1:
-            y_out[...] = jnp.transpose(yt[...]).astype(BF)
-    for piece in (2, 0, 3, 1):
-        pass_up(3, piece).wait_recv()
-        pass_down(3, piece).wait_recv()
-        value = pair_sum(0, piece)
-        value = value + ru_r[3, :, cols(piece)].astype(F32) + rd_r[3, :, cols(piece)].astype(F32)
-        gh_out[:, cols(piece)] = value.astype(BF)
-    for piece in range(PIECES):
-        swap(piece).wait_send()
-        for step in range(4):
-            if step > 0 or piece < HALF:
-                pass_up(step, piece).wait_send()
-            if step > 0 or piece >= HALF:
-                pass_down(step, piece).wait_send()
+        where = cols(quarter, count)
+        return own[at, where] + sbr[at, where].astype(F32)
+
+    def go_up(step, quarter, count):
+        value = pair_sum(4 - step, quarter, count)
+        if step > 1 or (step == 1 and quarter == 0):
+            for unit in quarters[:2] if step == 1 else ((quarter, count),):
+                pass_up(step - 1, *unit).wait_recv()
+            value = value + ru_r[step - 1, :, cols(quarter, count)].astype(F32)
+        ru_s[step, :, cols(quarter, count)] = value.astype(BF)
+        pass_up(step, quarter, count).start()
+
+    def go_down(step, quarter, count):
+        value = pair_sum(4 + step, quarter, count)
+        if step > 1 or (step == 1 and quarter == 2):
+            for unit in quarters[2:] if step == 1 else ((quarter, count),):
+                pass_down(step - 1, *unit).wait_recv()
+            value = value + rd_r[step - 1, :, cols(quarter, count)].astype(F32)
+        rd_s[step, :, cols(quarter, count)] = value.astype(BF)
+        pass_down(step, quarter, count).start()
+
+    def first_pass(quarter):
+        swap_far(quarter).wait_recv()
+        (go_up if quarter < 2 else go_down)(0, quarter, 1)
+
+    ready = None
+    for quarter in (0, 2, 1, 3):
+        multiply(quarter)
+        swap_far(quarter).start()
+        swap(quarter).start()
+        if ready is not None:
+            first_pass(ready)
+        ready = quarter
+    first_pass(ready)
+    for quarter in (2, 3):
+        swap(quarter).wait_recv()
+    go_up(1, 2, 2)
+    for quarter in (0, 1):
+        swap(quarter).wait_recv()
+    go_down(1, 0, 2)
+    go_up(1, 0, 2)
+    go_down(1, 2, 2)
+    y_out[...] = jnp.transpose(yt[...]).astype(BF)
+    for step in (2, 3):
+        go_up(step, 2, 2)
+        go_down(step, 0, 2)
+        go_up(step, 0, 2)
+        go_down(step, 2, 2)
+
+    def finish(quarter, up_here, down_here):
+        value = pair_sum(0, quarter, 2)
+        if up_here:
+            pass_up(3, quarter, 2).wait_recv()
+        if down_here:
+            pass_down(3, quarter, 2).wait_recv()
+        value = value + ru_r[3, :, cols(quarter, 2)].astype(F32)
+        value = value + rd_r[3, :, cols(quarter, 2)].astype(F32)
+        gh_out[:, cols(quarter, 2)] = value.astype(BF)
+
+    finish(2, True, True)
+    finish(0, True, True)
+
+    for step in range(4):
+        for unit in up_units[step]:
+            to_up(step, *unit).wait_send()
+        for unit in down_units[step]:
+            to_down(step, *unit).wait_send()
+    for place in range(PLANES):
+        for unit in twin_units.get(place, halves):
+            to_twin(place, *unit).wait_send()
+    for quarter in range(4):
+        swap_far(quarter).wait_send()
+        swap(quarter).wait_send()
+    for step in range(4):
+        for unit in quarters[:2] if step == 0 else halves:
+            pass_up(step, *unit).wait_send()
+        for unit in quarters[2:] if step == 0 else halves:
+            pass_down(step, *unit).wait_send()
     every(lambda step: out1(step).wait_send())
     every(lambda step: out2(step).wait_send())
 
@@ -518,24 +570,22 @@
     vmem = pl.BlockSpec(memory_space=pltpu.VMEM)
     smem = pl.BlockSpec(memory_space=pltpu.SMEM)
     dma = pltpu.SemaphoreType.DMA
+    whole = pl.BlockSpec(memory_space=pl.ANY)
     return pl.pallas_call(
         kernel,
         out_shape=(
-            jax.ShapeDtypeStruct((SPAN, XW), BF),
-            jax.ShapeDtypeStruct((ROWS, FEAT), BF),
+            pltpu.VMEM((SPAN, XW), BF),
+            pltpu.VMEM((ROWS, FEAT), BF),
         ),
-        in_specs=[vmem, pl.BlockSpec(memory_space=pl.ANY), vmem, smem, smem, smem, smem, vmem],
+        in_specs=[vmem, whole, vmem, smem, smem, smem, smem, vmem],
         out_specs=(vmem, vmem),
         scratch_shapes=[
-            pltpu.VMEM((FEAT, PROJ), BF),
-            pltpu.VMEM((128, FEAT), BF),
+            pltpu.VMEM((FEAT, WIDE), BF),
             pltpu.VMEM((SPAN, FEAT), BF),
-            pltpu.VMEM((SPAN, PROJ), F32),
-            pltpu.VMEM((SPAN, 128), F32),
+            pltpu.VMEM((SPAN, WIDE), F32),
             pltpu.VMEM((SPAN, SPAN), F32),
             pltpu.VMEM((XW, SPAN), BF),
-            pltpu.VMEM((SPAN, PROJ), F32),
-            pltpu.VMEM((SPAN, 128), F32),
+            pltpu.VMEM((SPAN, WIDE), F32),
             pltpu.VMEM((PROJ, SPAN), F32),
             pltpu.VMEM((PROJ, SPAN), F32),
             pltpu.VMEM((XW, SPAN), BF),
@@ -548,10 +598,8 @@
             pltpu.VMEM((SPANS, 2 * PART + 16, STATE), BF),
             pltpu.VMEM((SPANS, 2 * PART, STATE), BF),
             pltpu.VMEM((SPANS, 2 * PART, STATE), BF),
-            pltpu.VMEM((PROJ, SPAN), F32),
-            pltpu.VMEM((128, SPAN), F32),
-            pltpu.VMEM((SPAN, PROJ), BF),
-            pltpu.VMEM((SPAN, 128), BF),
+            pltpu.VMEM((WIDE, SPAN), F32),
+            pltpu.VMEM((SPAN, WIDE), BF),
             pltpu.VMEM((128, FEAT), F32),
             pltpu.VMEM((128, FEAT), BF),
             pltpu.VMEM((128, FEAT), BF),
@@ -560,14 +608,14 @@
             pltpu.VMEM((4, ROWS, FEAT), BF),
             pltpu.VMEM((4, ROWS, FEAT), BF),
             dma,
-            dma((4, PIECES)), dma((4, PIECES)), dma((4, PIECES)), dma((4, PIECES)),
-            dma((PLANES, PIECES)), dma((PLANES, PIECES)),
+            dma((4, 4)), dma((4, 4)), dma((4, 4)), dma((4, 4)),
+            dma((PLANES, 4)), dma((PLANES, 4)),
             dma((SPANS,)), dma((SPANS,)), dma((SPANS,)), dma((SPANS,)),
-            dma((4, PIECES)), dma((4, PIECES)), dma((4, PIECES)), dma((4, PIECES)),
-            dma((PIECES,)), dma((PIECES,)),
+            dma((4, 4)), dma((4, 4)), dma((4, 4)), dma((4, 4)),
+            dma((4,)), dma((4,)), dma((4,)), dma((4,)),
         ],
         compiler_params=pltpu.CompilerParams(
-            collective_id=0, has_side_effects=True, vmem_limit_bytes=60 * 1024 * 1024
+            collective_id=0, has_side_effects=True, vmem_limit_bytes=58 * 1024 * 1024
         ),
         name="layer",
     )(hidden, w_proj, w_dt, dt_bias, a_log, d_skip, doc_lengths, grad_out)

time: 90 us -> 83.4 us (0.927)
  Pallas kernels: 85.9 us -> 81.3 us
  local copies, waits for them, and re-layouts: 3.34 us -> 1.41 us
    pallas_call x1, Pallas kernels: 85.9 us -> 81.3 us  [per_device(): pl.pallas_call(kernel, out_shape=(pltpu.VMEM((SPAN, XW), BF), pltpu.VMEM(...]
    unnamed x2, local copies, waits for them, and re-layouts: 3.34 us -> 1.41 us
where the time goes in v2:
time: 83.4 us; the launch traced here: 83.3 us
  Pallas kernels  81.3 us (97%)
  local copies, waits for them, and re-layouts  1.41 us (2%)
    pallas_call x1, Pallas kernels, per_device(): pl.pallas_call(kernel, out_shape=(pltpu.VMEM((SPAN, XW), BF), pltpu.VMEM(...  81.3 us

profile of v2, /device:TPU:1, one launch (start us, length us, event | category | flops | bytes accessed | tf_op | source)
XLA Modules:
  0.0 83.3 jit_solution(198918705282192562)
XLA Ops:
  0.6 81.3 %layer.1 = (bf16[256,512]{1,0:T(8,128)(2,1)S(1)}, bf16[16,8192]{1,0:T(8,128)(2,1)S(1)}) custom-call(bf16[16,8192]{1,0:T(8,128)(2,1)} %hid.1, bf16[8192,768]{1,0:T(8,128)(2,1)} %w_hbm.1, bf16[8,8192]{1,0:T(8,128)(2,1)} %wdt_ref.1, f32[8]{0:T(128)} %bias_ref.1, f32[8]{0:T(128)} %alog_ref.1, f32[8]{0:T(128)} %skip_ref.1, s32[8]{0:T(128)} %docs.1, ...), custom_call_target="tpu_custom_call" | custom-call | tf_op jit(solution)/shard_map/layer/pallas_call | solution.py:574
  81.9 0.7 copy.12
  82.6 0.7 copy.13

commit v3 on v2

v3 whole, which is shorter than its diff:
```python
import jax
import jax.numpy as jnp
from jax import lax
from jax.experimental import pallas as pl
from jax.experimental.pallas import tpu as pltpu
from jax.sharding import PartitionSpec as P

BF = jnp.bfloat16
F32 = jnp.float32
MESH = pl.DeviceIdType.MESH

PLANES = 8
SPANS = 16
ROWS = 16
SPAN = 256
FEAT = 8192
HEADS = 8
HDIM = 64
XW = HEADS * HDIM
STATE = 128
PROJ = XW + 2 * STATE
WIDE = PROJ + 128
QUARTER = FEAT // 4
PART = XW // SPANS
SLOT = {0: 0, 1: 1, 7: 2, 2: 3, 6: 4, 3: 5, 5: 6, 4: 7}
NEAR = 5 * 32

NN = (((1,), (0,)), ((), ()))
NT = (((1,), (1,)), ((), ()))
TN = (((0,), (0,)), ((), ()))


def mm(a, b, dims=NN):
    return lax.dot_general(a, b, dims, preferred_element_type=F32)


def cols(quarter, count=1):
    return pl.ds(quarter * QUARTER, count * QUARTER)


def quantize(rows):
    lane = lax.broadcasted_iota(jnp.int32, rows.shape, 1)
    largest = jnp.abs(rows)
    for step in (1, 2, 4, 8, 16):
        below = pltpu.roll(largest, step, 1)
        above = pltpu.roll(largest, 128 - step, 1)
        largest = jnp.maximum(largest, jnp.where((lane & step) != 0, below, above))
    power = jnp.exp2(jnp.floor(jnp.log2(jnp.maximum(largest, 2.0**-39)))).astype(BF).astype(F32)
    power = jnp.where(power > largest, power * 0.5, power)
    power = jnp.where(power * 2.0 <= largest, power * 2.0, power)
    scale = jnp.where(largest >= 2.0**-39, power * 2.0**-8, 2.0**-48)
    lifted = rows * 2.0**20
    normal = (rows + lifted) - lifted
    anchor = scale * (1.5 * 2.0**14)
    small = (rows + anchor) - anchor
    snapped = jnp.where(jnp.abs(rows) < scale * 2.0**-6, small, normal)
    bound = scale * 448.0
    return jnp.clip(snapped, -bound, bound)


def split3(values):
    first = values.astype(BF)
    rest = values - first.astype(F32)
    second = rest.astype(BF)
    third = (rest - second.astype(F32)).astype(BF)
    return first, second, third


def sums(values, chosen):
    first, second, third = split3(values)
    stacked = jnp.concatenate(
        [first.astype(F32), second.astype(F32), third.astype(F32), jnp.zeros_like(values)], axis=0
    ).astype(BF)
    out = mm(stacked, chosen)
    return out[0:8] + out[8:16] + out[16:24]


def head_lanes(scalars):
    lane = lax.broadcasted_iota(jnp.int32, (8, 128), 1)
    out = jnp.zeros((8, 128), F32)
    for head in range(HEADS):
        out = jnp.where(lane == head, scalars[head], out)
    return out


def split2(values):
    high = values.astype(BF)
    return high, (values - high.astype(F32)).astype(BF)


def spread(values, spreader):
    return mm(jnp.concatenate(split2(values), axis=1), spreader)


def head_rows(head):
    return pl.ds(head * HDIM, HDIM)


def kernel(
    hid, w_hbm, wdt_ref, bias_ref, alog_ref, skip_ref, docs, go,
    y_out, gh_out,
    w, wt, xb, acc, bias_m, masks, spreader, gyt, pn, dn_, xn, dstn, bc, dte, kdd, crw, xk, ku, gw,
    ut, yt, dut, ds_, yn, pre, dbc, xs, xr, os_, or_, pgn, pga, sbr, ru_r, rd_r,
    wsem, au_s, au_r, ad_s, ad_r, ab_s, ab_r, x1s, x1r, x2s, x2r,
    bu_s, bu_r, bd_s, bd_r, bb_s, bb_r, bf_s, bf_r, bn_s, bn_r, heard,
):
    me = lax.axis_index("tensor")
    span = lax.axis_index("context")
    z = me // 2
    core = me % 2
    up = lax.rem(z + 1, PLANES) * 2 + core
    down = lax.rem(z + PLANES - 1, PLANES) * 2 + core
    twin = z * 2 + (1 - core)

    w_copy = pltpu.make_async_copy(w_hbm, w.at[:, 0:PROJ], wsem)
    w_copy.start()

    barrier = pltpu.get_barrier_semaphore()
    for near in (up, down, twin):
        pl.semaphore_signal(barrier, inc=1, device_id={"tensor": near}, device_id_type=MESH)

    x, y = span % 4, span // 4
    beside = (y * 4 + lax.rem(x + 1, 4), y * 4 + lax.rem(x + 3, 4))
    across = (lax.rem(y + 1, 4) * 4 + x, lax.rem(y + 3, 4) * 4 + x)
    for near in beside + across:
        pl.semaphore_signal(barrier, inc=1, device_id={"context": near}, device_id_type=MESH)

    def tell(whom, sem):
        for near in whom:
            pl.semaphore_signal(sem, inc=1, device_id={"context": near}, device_id_type=MESH)

    def block(place, half, quarter, count):
        return xb.at[pl.ds(SLOT[place % PLANES] * 32 + half * 16, ROWS), cols(quarter, count)]

    def to_up(step, quarter, count):
        return pltpu.make_async_remote_copy(
            src_ref=block(-step, 0, quarter, count), dst_ref=block(-step - 1, 0, quarter, count),
            send_sem=au_s.at[step, quarter], recv_sem=au_r.at[step, quarter],
            device_id={"tensor": up}, device_id_type=MESH,
        )

    def to_down(step, quarter, count):
        return pltpu.make_async_remote_copy(
            src_ref=block(step, 0, quarter, count), dst_ref=block(step + 1, 0, quarter, count),
            send_sem=ad_s.at[step, quarter], recv_sem=ad_r.at[step, quarter],
            device_id={"tensor": down}, device_id_type=MESH,
        )

    def to_twin(place, quarter, count):
        place = place % PLANES
        return pltpu.make_async_remote_copy(
            src_ref=block(place, 0, quarter, count), dst_ref=block(place, 1, quarter, count),
            send_sem=ab_s.at[place, quarter], recv_sem=ab_r.at[place, quarter],
            device_id={"tensor": twin}, device_id_type=MESH,
        )

    quarters = ((0, 1), (1, 1), (2, 1), (3, 1))
    halves = ((0, 2), (2, 2))
    up_units = (quarters, halves, halves, quarters[:2])
    down_units = (quarters[2:] + quarters[:2], halves[::-1], halves[::-1], quarters[2:])
    twin_units = {0: ((0, 4),), 4: quarters}

    tiles = QUARTER // 128

    def encode(quarter):
        part = hid[:, quarter * QUARTER : (quarter + 1) * QUARTER].astype(F32)
        stacked = jnp.concatenate(
            [part[:, i * 128 : (i + 1) * 128] for i in range(tiles)], axis=0
        )
        snapped = quantize(stacked)
        flat = jnp.concatenate(
            [snapped[i * ROWS : (i + 1) * ROWS] for i in range(tiles)], axis=1
        )
        xb[0:ROWS, quarter * QUARTER : (quarter + 1) * QUARTER] = flat.astype(BF)

    encode(0)
    pl.semaphore_wait(barrier, 7)
    to_up(0, 0, 1).start()
    encode(2)
    to_down(0, 2, 1).start()
    encode(1)
    to_up(0, 1, 1).start()
    encode(3)
    to_down(0, 3, 1).start()
    to_up(0, 2, 1).start()
    to_down(0, 0, 1).start()
    to_up(0, 3, 1).start()
    to_down(0, 1, 1).start()
    to_twin(0, 0, 4).start()
    tell(beside, heard.at[0])

    first_token = span * SPAN

    def segment(positions):
        out = jnp.full(positions.shape, -1, jnp.int32)
        begin = jnp.int32(0)
        for doc in range(8):
            out = out + jnp.where(positions >= begin, 1, 0)
            begin = begin + docs[doc]
        return out

    row_pos = first_token + lax.broadcasted_iota(jnp.int32, (SPAN, SPAN), 0)
    col_pos = first_token + lax.broadcasted_iota(jnp.int32, (SPAN, SPAN), 1)
    bias_m[...] = jnp.where(
        (row_pos >= col_pos) & (segment(row_pos) == segment(col_pos)), 0.0, -1e30
    )
    token = first_token + lax.broadcasted_iota(jnp.int32, (SPAN, 128), 0)
    seg = segment(token)
    none = jnp.zeros((8, 128), jnp.int32)
    seg_before = segment(none + (first_token - 1))
    seg_last = segment(none + (first_token + SPAN - 1))
    masks[0] = jnp.where(seg == seg_before[0:1], 1.0, 0.0)
    masks[1] = jnp.where(seg == seg_last[0:1], 1.0, 0.0)
    through = jnp.where(seg_last == seg_before, 1.0, 0.0)
    head_of_row = lax.rem(lax.broadcasted_iota(jnp.int32, (256, XW), 0), 128)
    head_of_lane = lax.broadcasted_iota(jnp.int32, (256, XW), 1) // HDIM
    spreader[...] = jnp.where(head_of_row == head_of_lane, 1.0, 0.0).astype(BF)
    gyt[...] = jnp.transpose(go[...].astype(F32)).astype(BF)

    for quarter in range(4):
        steps_w = wdt_ref[:, quarter * QUARTER : (quarter + 1) * QUARTER].astype(F32)
        padded = jnp.concatenate([steps_w, jnp.zeros((120, QUARTER), F32)], axis=0)
        w[cols(quarter), PROJ:WIDE] = jnp.transpose(padded).astype(BF)
        wt[PROJ:WIDE, cols(quarter)] = padded.astype(BF)
    square_row = lax.broadcasted_iota(jnp.int32, (256, 256), 0)
    square_lane = lax.broadcasted_iota(jnp.int32, (256, 256), 1)
    same = jnp.where(square_row == square_lane, 1.0, 0.0).astype(BF)
    units = [(quarter, first) for quarter in (0, 2, 1, 3) for first in range(0, PROJ, 256)]

    def turn_weights(count):
        for _ in range(count):
            quarter, first = units.pop(0)
            at = slice(first, first + 256)
            wt[at, cols(quarter)] = mm(same, w[cols(quarter), at], NT).astype(BF)

    def project(first, last, quarter, begin):
        at = slice(quarter * QUARTER, (quarter + 1) * QUARTER)
        part = mm(xb[first:last, at], w[at, :])
        if begin:
            acc[first:last, :] = part
        else:
            acc[first:last, :] += part

    def arrived_twin(place):
        for unit in twin_units.get(place, halves):
            to_twin(place, *unit).wait_recv()

    def between(step, turn):
        if (step, turn) == (0, 0):
            pl.semaphore_wait(heard.at[0], 2)
            tell(across, heard.at[1])
            w_copy.wait()
            turn_weights(3)
        elif (step, turn) == (0, 1):
            pl.semaphore_wait(heard.at[1], 2)
            tell(across, heard.at[2])
            turn_weights(3)
        elif (step, turn) == (1, 0):
            pl.semaphore_wait(heard.at[2], 2)
            turn_weights(4)
        elif (step, turn) == (1, 1):
            turn_weights(2)
            for place in (0, 1, 7, 2, 6):
                arrived_twin(place)
            project(0, NEAR, 0, True)
            project(0, NEAR, 1, False)
        elif (step, turn) == (2, 0):
            project(0, NEAR, 2, False)
            project(0, NEAR, 3, False)

    for step in range(3):
        for turn in range(2):
            unit = halves[turn]
            for got in quarters[2 * turn : 2 * turn + 2] if step == 0 else (unit,):
                to_up(step, *got).wait_recv()
            if step < 2:
                to_up(step + 1, *unit).start()
            elif turn == 0:
                for part in up_units[3]:
                    to_up(3, *part).start()
            to_twin(-step - 1, *unit).start()
            unit = halves[1 - turn]
            for got in quarters[2 - 2 * turn : 4 - 2 * turn] if step == 0 else (unit,):
                to_down(step, *got).wait_recv()
            if step < 2:
                to_down(step + 1, *unit).start()
            elif turn == 0:
                for part in down_units[3]:
                    to_down(3, *part).start()
            to_twin(step + 1, *unit).start()
            between(step, turn)
    for at in range(2):
        to_up(3, *up_units[3][at]).wait_recv()
        to_twin(4, *up_units[3][at]).start()
        to_down(3, *down_units[3][at]).wait_recv()
        to_twin(4, *down_units[3][at]).start()
    arrived_twin(3)
    arrived_twin(5)
    for quarter in (0, 2, 1, 3):
        to_twin(4, quarter, 1).wait_recv()
        project(NEAR, SPAN, quarter, quarter == 0)

    def home(place, half):
        owner = lax.rem(z + place, PLANES) * 2 + (core if half == 0 else 1 - core)
        return pl.ds(pl.multiple_of(owner * ROWS, ROWS), ROWS)

    for place in range(PLANES):
        for half in range(2):
            at = SLOT[place] * 32 + half * 16
            pn[home(place, half), :] = acc[at : at + 16, 0:PROJ].astype(BF).astype(F32)
            dn_[home(place, half), :] = acc[at : at + 16, PROJ:WIDE]

    row = lax.broadcasted_iota(jnp.int32, (SPAN, SPAN), 0)
    lane = lax.broadcasted_iota(jnp.int32, (SPAN, SPAN), 1)
    rate = -jnp.exp(head_lanes(alog_ref))
    skip = head_lanes(skip_ref)
    dt_arg = dn_[...] + head_lanes(bias_ref)[0:1]
    dt = jnp.maximum(dt_arg, 0.0) + jnp.log1p(jnp.exp(-jnp.abs(dt_arg)))
    dt_gate = 1.0 / (1.0 + jnp.exp(-dt_arg))
    summed = mm(
        jnp.where(row >= lane, 1.0, 0.0).astype(BF),
        jnp.concatenate(split3(dt * rate[0:1]), axis=1),
    )
    cum = summed[:, 0:128] + summed[:, 128:256] + summed[:, 256:384]
    cum_last = cum[SPAN - 1 : SPAN]
    carry_w = jnp.exp(cum) * masks[0]
    keep_w = jnp.exp(cum_last - cum) * masks[1]
    total = jnp.exp(jnp.broadcast_to(cum_last, (8, 128))) * through
    keep_dt = spread(keep_w * dt, spreader[...])
    crw[...] = spread(carry_w, spreader[...])
    projected = pn[...]
    gate = 1.0 / (1.0 + jnp.exp(-projected))
    dstn[...] = gate * (1.0 + projected * (1.0 - gate))
    active = projected * gate
    xn[...] = active[:, 0:XW]
    bc[...] = active[:, XW:PROJ].astype(BF)
    b_nat = bc[:, 0:STATE]
    c_nat = bc[:, STATE : 2 * STATE]
    b_t = jnp.transpose(active[:, XW : XW + STATE]).astype(BF)
    c_t = jnp.transpose(active[:, XW + STATE : PROJ]).astype(BF)
    ku[...] = (xn[...] * keep_dt).astype(BF)
    gw[...] = (go[...].astype(F32) * crw[...]).astype(BF)
    end_state = mm(b_t, ku[...]).astype(BF)
    from_out = mm(c_t, gw[...]).astype(BF)
    note_row = lax.broadcasted_iota(jnp.int32, (16, 128), 0)
    high, low_part = split2(total[0:1])
    note = jnp.where(note_row == 0, high.astype(F32), jnp.where(note_row == 1, low_part.astype(F32), 0.0))
    note = mm(note.astype(BF), spreader[0:128, :]).astype(BF)
    for part in range(SPANS):
        at = slice(part % 4 * PART, part % 4 * PART + PART)
        pair = slice(part // 4 * 128, part // 4 * 128 + 128)
        xs[part, 0:PART, :] = end_state[at, pair]
        xs[part, PART : 2 * PART, :] = from_out[at, pair]
        xs[part, 2 * PART : 2 * PART + 16, :] = note[:, pair]

    def other(step):
        return lax.rem(span + step, SPANS)

    def out1(step):
        return pltpu.make_async_remote_copy(
            src_ref=xs.at[other(step)], dst_ref=xr.at[span],
            send_sem=x1s.at[other(step)], recv_sem=x1r.at[span],
            device_id={"context": other(step)}, device_id_type=MESH,
        )

    def in1(step):
        return pltpu.make_async_remote_copy(
            src_ref=xs.at[other(step)], dst_ref=xr.at[other(step)],
            send_sem=x1s.at[other(step)], recv_sem=x1r.at[other(step)],
            device_id={"context": other(step)}, device_id_type=MESH,
        )

    def out2(step):
        return pltpu.make_async_remote_copy(
            src_ref=os_.at[other(step)], dst_ref=or_.at[span],
            send_sem=x2s.at[other(step)], recv_sem=x2r.at[span],
            device_id={"context": other(step)}, device_id_type=MESH,
        )

    def in2(step):
        return pltpu.make_async_remote_copy(
            src_ref=os_.at[other(step)], dst_ref=or_.at[other(step)],
            send_sem=x2s.at[other(step)], recv_sem=x2r.at[other(step)],
            device_id={"context": other(step)}, device_id_type=MESH,
        )

    def every(action):
        for step in (10, 9, 11, 6, 14, 8, 2, 5, 7, 13, 15, 4, 12, 1, 3):
            action(step)

    every(lambda step: out1(step).start())
    xr[span] = xs[span]

    dte[...] = spread(dt, spreader[...])
    xk[...] = (xn[...] * spread(keep_w, spreader[...])).astype(BF)
    kdd[...] = keep_dt * dstn[:, 0:XW]
    ut[...] = jnp.transpose(xn[...] * dte[...]).astype(BF)
    cum_row = jnp.transpose(cum)
    scores = mm(c_nat, b_t)
    low = jnp.where(lax.broadcasted_iota(jnp.int32, (1, 128), 1) < HDIM, 1.0, 0.0).astype(BF)
    high_half = jnp.where(lax.broadcasted_iota(jnp.int32, (1, 128), 1) < HDIM, 0.0, 1.0).astype(BF)

    def inner(head):
        at = head_rows(head)
        pair = head // 2 * 128
        gap = cum[:, head : head + 1] - cum_row[head : head + 1, :] + bias_m[...]
        decay = jnp.exp(gap)
        mixing = (scores * decay).astype(BF)
        yt[at, :] = mm(ut[at, :], mixing, NT)
        dut[at, :] = mm(gyt[at, :], mixing)
        picked = go[:, pair : pair + 128] * (low if head % 2 == 0 else high_half)
        products = mm(picked, ut[pair : pair + 128, :])
        if head == 0:
            ds_[...] = products * decay
        else:
            ds_[...] += products * decay

    for head in range(HEADS // 2):
        inner(head)

    every(lambda step: in1(step).wait_recv())
    forward = jnp.zeros((PART, STATE), F32)
    back = jnp.zeros((PART, STATE), F32)
    for source in range(SPANS):
        os_[source, 0:PART, :] = forward.astype(BF)
        decays = xr[source, 2 * PART : 2 * PART + 16, :].astype(F32)
        forward = (decays[0:1] + decays[1:2]) * forward + xr[source, 0:PART, :].astype(F32)
        later = SPANS - 1 - source
        os_[later, PART : 2 * PART, :] = back.astype(BF)
        decays = xr[later, 2 * PART : 2 * PART + 16, :].astype(F32)
        back = (decays[0:1] + decays[1:2]) * back + xr[later, PART : 2 * PART, :].astype(F32)
    every(lambda step: out2(step).start())
    or_[span] = os_[span]

    for head in range(HEADS // 2, HEADS):
        inner(head)
    ds = ds_[...].astype(BF)
    dbc[:, 0:STATE] = mm(ds, c_nat, TN)
    dbc[:, STATE : 2 * STATE] = mm(ds, b_nat)
    gap_grad, direct = [], []
    for head in range(HEADS):
        at = head_rows(head)
        x_dt = ut[at, :].astype(F32)
        gap_grad.append(
            jnp.sum(gyt[at, :].astype(F32) * yt[at, :] - x_dt * dut[at, :], axis=0, keepdims=True)
        )
    yn[...] = jnp.transpose(yt[...])
    du_here = jnp.transpose(dut[...])
    skip_all = spread(skip, spreader[...])[0:1]
    x_here = xn[...]
    given = go[...].astype(F32)
    pre[...] = (du_here * dte[...] + given * skip_all) * dstn[:, 0:XW]
    yn[...] = yn[...] + x_here * skip_all
    direct = mm(
        jnp.concatenate(split2(x_here * du_here), axis=0), spreader[0:128, :], NT
    )
    direct = direct[0:SPAN] + direct[SPAN : 2 * SPAN]
    log_rows = sums(
        jnp.concatenate(gap_grad, axis=0), jnp.where(row >= lane, 1.0, 0.0).astype(BF)
    )
    log_here = jnp.transpose(
        jnp.concatenate([log_rows, jnp.zeros((120, SPAN), F32)], axis=0)
    )
    since_before = jnp.concatenate(
        [jnp.where(row <= lane, 1.0, 0.0).astype(BF), jnp.where(row > lane, 1.0, 0.0).astype(BF)],
        axis=1,
    )

    every(lambda step: in2(step).wait_recv())

    def gathered(first):
        return jnp.concatenate(
            [
                jnp.concatenate(
                    [or_[pair * 4 + part, first : first + PART, :] for part in range(4)], axis=0
                )
                for pair in range(4)
            ],
            axis=1,
        )

    state_in = gathered(0)
    state_grad = gathered(PART)
    carried = mm(c_nat, state_in)
    reach = mm(b_nat, state_grad)
    pgn[:, 0:XW] = (pre[...] + reach * kdd[...]).astype(BF)
    db = dbc[:, 0:STATE] + mm(ku[...], state_grad, NT)
    dc = dbc[:, STATE : 2 * STATE] + mm(gw[...], state_in, NT)
    pgn[:, XW : XW + STATE] = (db * dstn[:, XW : XW + STATE]).astype(BF)
    pgn[:, XW + STATE : PROJ] = (dc * dstn[:, XW + STATE : PROJ]).astype(BF)
    ends = jnp.sum(
        (state_in.astype(F32) * state_grad.astype(F32)).reshape(STATE // 8, 8, XW), axis=0
    )
    products = jnp.concatenate(
        [
            (gw[...].astype(F32) * carried).astype(BF),
            (ku[...].astype(F32) * reach).astype(BF),
            (xk[...].astype(F32) * reach).astype(BF),
            jnp.concatenate(split2(jnp.concatenate([ends, ends], axis=0)), axis=0),
        ],
        axis=0,
    )
    reduced = mm(products, spreader[0:128, :], NT)
    far_grad = mm(
        since_before, jnp.concatenate(split2(reduced[0 : 2 * SPAN]), axis=1)
    )
    far_grad = far_grad[:, 0:128] + far_grad[:, 128:256]
    end_grad = reduced[3 * SPAN : 3 * SPAN + 8] + reduced[3 * SPAN + 16 : 3 * SPAN + 24]
    end_grad = jnp.sum(end_grad, axis=0, keepdims=True)
    log_grad = log_here + far_grad + total[0:1] * end_grad
    dt_grad = (direct + reduced[2 * SPAN : 3 * SPAN] + rate[0:1] * log_grad) * dt_gate
    pgn[:, PROJ:WIDE] = dt_grad.astype(BF)
    yn[...] = yn[...] + carried * crw[...]

    for step in range(4):
        for unit in up_units[step]:
            to_up(step, *unit).wait_send()
        for unit in down_units[step]:
            to_down(step, *unit).wait_send()
    for place in range(PLANES):
        for unit in twin_units.get(place, halves):
            to_twin(place, *unit).wait_send()
    own, sbs = xb.at[0:128, :], xb.at[128:256, :]
    for place in range(PLANES):
        for half in range(2):
            at = half * 128 + SLOT[place] * 16
            pga[at : at + 16, :] = pgn[home(place, half), :]

    def multiply(quarter):
        term = mm(pga[...], wt[:, cols(quarter)]).astype(BF)
        own[:, cols(quarter)] = term[0:128]
        sbs[:, cols(quarter)] = term[128:256]

    def swap(quarter, first, last, sems):
        return pltpu.make_async_remote_copy(
            src_ref=sbs.at[first:last, cols(quarter)], dst_ref=sbr.at[first:last, cols(quarter)],
            send_sem=sems[0].at[quarter], recv_sem=sems[1].at[quarter],
            device_id={"tensor": twin}, device_id_type=MESH,
        )

    def swap_far(quarter):
        return swap(quarter, 112, 128, (bf_s, bf_r))

    def swap_next(quarter):
        return swap(quarter, 80, 112, (bn_s, bn_r))

    def swap_rest(quarter):
        return swap(quarter, 0, 80, (bb_s, bb_r))

    def place_rows(place):
        return pl.ds(SLOT[place % PLANES] * 16, 16)

    def pass_up(step, quarter, count):
        return pltpu.make_async_remote_copy(
            src_ref=own.at[place_rows(4 - step), cols(quarter, count)], dst_ref=ru_r.at[step, :, cols(quarter, count)],
            send_sem=bu_s.at[step, quarter], recv_sem=bu_r.at[step, quarter],
            device_id={"tensor": up}, device_id_type=MESH,
        )

    def pass_down(step, quarter, count):
        return pltpu.make_async_remote_copy(
            src_ref=own.at[place_rows(4 + step), cols(quarter, count)], dst_ref=rd_r.at[step, :, cols(quarter, count)],
            send_sem=bd_s.at[step, quarter], recv_sem=bd_r.at[step, quarter],
            device_id={"tensor": down}, device_id_type=MESH,
        )

    def pair_sum(place, quarter, count):
        at = place_rows(place)
        where = cols(quarter, count)
        return own[at, where].astype(F32) + sbr[at, where].astype(F32)

    def go_up(step, quarter, count):
        value = pair_sum(4 - step, quarter, count)
        if step > 1 or (step == 1 and quarter == 0):
            for unit in quarters[:2] if step == 1 else ((quarter, count),):
                pass_up(step - 1, *unit).wait_recv()
            value = value + ru_r[step - 1, :, cols(quarter, count)].astype(F32)
        own[place_rows(4 - step), cols(quarter, count)] = value.astype(BF)
        pass_up(step, quarter, count).start()

    def go_down(step, quarter, count):
        value = pair_sum(4 + step, quarter, count)
        if step > 1 or (step == 1 and quarter == 2):
            for unit in quarters[2:] if step == 1 else ((quarter, count),):
                pass_down(step - 1, *unit).wait_recv()
            value = value + rd_r[step - 1, :, cols(quarter, count)].astype(F32)
        own[place_rows(4 + step), cols(quarter, count)] = value.astype(BF)
        pass_down(step, quarter, count).start()

    def first_pass(quarter):
        swap_far(quarter).wait_recv()
        (go_up if quarter < 2 else go_down)(0, quarter, 1)

    for quarter in (0, 2, 1, 3):
        multiply(quarter)
        swap_far(quarter).start()
        swap_next(quarter).start()
    for quarter in (0, 2, 1, 3):
        swap_rest(quarter).start()
    for quarter in (0, 2, 1, 3):
        first_pass(quarter)
    for quarter in (2, 3):
        swap_next(quarter).wait_recv()
    go_up(1, 2, 2)
    for quarter in (0, 1):
        swap_next(quarter).wait_recv()
    go_down(1, 0, 2)
    go_up(1, 0, 2)
    go_down(1, 2, 2)
    for quarter in range(4):
        swap_rest(quarter).wait_recv()
    y_out[...] = yn[...].astype(BF)
    for step in (2, 3):
        go_up(step, 2, 2)
        go_down(step, 0, 2)
        go_up(step, 0, 2)
        go_down(step, 2, 2)

    def finish(quarter, up_here, down_here):
        value = pair_sum(0, quarter, 2)
        if up_here:
            pass_up(3, quarter, 2).wait_recv()
        if down_here:
            pass_down(3, quarter, 2).wait_recv()
        value = value + ru_r[3, :, cols(quarter, 2)].astype(F32)
        value = value + rd_r[3, :, cols(quarter, 2)].astype(F32)
        gh_out[:, cols(quarter, 2)] = value.astype(BF)

    finish(2, True, True)
    finish(0, True, True)

    for quarter in range(4):
        swap_far(quarter).wait_send()
        swap_next(quarter).wait_send()
        swap_rest(quarter).wait_send()
    for step in range(4):
        for unit in quarters[:2] if step == 0 else halves:
            pass_up(step, *unit).wait_send()
        for unit in quarters[2:] if step == 0 else halves:
            pass_down(step, *unit).wait_send()
    every(lambda step: out1(step).wait_send())
    every(lambda step: out2(step).wait_send())


def per_device(hidden, w_proj, w_dt, dt_bias, a_log, d_skip, doc_lengths, grad_out):
    vmem = pl.BlockSpec(memory_space=pltpu.VMEM)
    smem = pl.BlockSpec(memory_space=pltpu.SMEM)
    dma = pltpu.SemaphoreType.DMA
    whole = pl.BlockSpec(memory_space=pl.ANY)
    return pl.pallas_call(
        kernel,
        out_shape=(
            pltpu.VMEM((SPAN, XW), BF),
            pltpu.VMEM((ROWS, FEAT), BF),
        ),
        in_specs=[vmem, whole, vmem, smem, smem, smem, smem, vmem],
        out_specs=(vmem, vmem),
        scratch_shapes=[
            pltpu.VMEM((FEAT, WIDE), BF),
            pltpu.VMEM((WIDE, FEAT), BF),
            pltpu.VMEM((SPAN, FEAT), BF),
            pltpu.VMEM((SPAN, WIDE), F32),
            pltpu.VMEM((SPAN, SPAN), F32),
            pltpu.VMEM((2, SPAN, 128), F32),
            pltpu.VMEM((256, XW), BF),
            pltpu.VMEM((XW, SPAN), BF),
            pltpu.VMEM((SPAN, PROJ), F32),
            pltpu.VMEM((SPAN, 128), F32),
            pltpu.VMEM((SPAN, XW), F32),
            pltpu.VMEM((SPAN, PROJ), F32),
            pltpu.VMEM((SPAN, 2 * STATE), BF),
            pltpu.VMEM((SPAN, XW), F32),
            pltpu.VMEM((SPAN, XW), F32),
            pltpu.VMEM((SPAN, XW), F32),
            pltpu.VMEM((SPAN, XW), BF),
            pltpu.VMEM((SPAN, XW), BF),
            pltpu.VMEM((SPAN, XW), BF),
            pltpu.VMEM((XW, SPAN), BF),
            pltpu.VMEM((XW, SPAN), F32),
            pltpu.VMEM((XW, SPAN), F32),
            pltpu.VMEM((SPAN, SPAN), F32),
            pltpu.VMEM((SPAN, XW), F32),
            pltpu.VMEM((SPAN, XW), F32),
            pltpu.VMEM((SPAN, 2 * STATE), F32),
            pltpu.VMEM((SPANS, 2 * PART + 16, STATE), BF),
            pltpu.VMEM((SPANS, 2 * PART + 16, STATE), BF),
            pltpu.VMEM((SPANS, 2 * PART, STATE), BF),
            pltpu.VMEM((SPANS, 2 * PART, STATE), BF),
            pltpu.VMEM((SPAN, WIDE), BF),
            pltpu.VMEM((SPAN, WIDE), BF),
            pltpu.VMEM((128, FEAT), BF),
            pltpu.VMEM((4, ROWS, FEAT), BF),
            pltpu.VMEM((4, ROWS, FEAT), BF),
            dma,
            dma((4, 4)), dma((4, 4)), dma((4, 4)), dma((4, 4)),
            dma((PLANES, 4)), dma((PLANES, 4)),
            dma((SPANS,)), dma((SPANS,)), dma((SPANS,)), dma((SPANS,)),
            dma((4, 4)), dma((4, 4)), dma((4, 4)), dma((4, 4)),
            dma((4,)), dma((4,)), dma((4,)), dma((4,)), dma((4,)), dma((4,)),
            pltpu.SemaphoreType.REGULAR((3,)),
        ],
        compiler_params=pltpu.CompilerParams(
            collective_id=0, has_side_effects=True, vmem_limit_bytes=58 * 1024 * 1024
        ),
        name="layer",
    )(hidden, w_proj, w_dt, dt_bias, a_log, d_skip, doc_lengths, grad_out)


def solution(mesh):
    placed = (
        P(("context", "tensor"), None),
        P(None, "tensor"),
        P("tensor", None),
        P("tensor"),
        P("tensor"),
        P("tensor"),
        P(),
        P("context", "tensor"),
    )
    return jax.shard_map(
        per_device,
        mesh=mesh,
        in_specs=placed,
        out_specs=(P("context", "tensor"), P(("context", "tensor"), None)),
        check_vma=False,
    )
```

time: 83.4 us -> 81.4 us (0.976)
  Pallas kernels: 81.3 us -> 79.3 us
    pallas_call x1, Pallas kernels: 81.3 us -> 79.3 us  [per_device(): pl.pallas_call(kernel, out_shape=(pltpu.VMEM((SPAN, XW), BF), pltpu.VMEM(...]
where the time goes in v3:
time: 81.4 us; the launch traced here: 81.3 us
  Pallas kernels  79.3 us (97%)
  local copies, waits for them, and re-layouts  1.41 us (2%)
    pallas_call x1, Pallas kernels, per_device(): pl.pallas_call(kernel, out_shape=(pltpu.VMEM((SPAN, XW), BF), pltpu.VMEM(...  79.3 us

profile of v3, /device:TPU:1, one launch (start us, length us, event | category | flops | bytes accessed | tf_op | source)
XLA Modules:
  0.0 81.3 jit_solution(6088677083465602016)
XLA Ops:
  0.6 79.3 %layer.1 = (bf16[256,512]{1,0:T(8,128)(2,1)S(1)}, bf16[16,8192]{1,0:T(8,128)(2,1)S(1)}) custom-call(bf16[16,8192]{1,0:T(8,128)(2,1)} %hid.1, bf16[8192,768]{1,0:T(8,128)(2,1)} %w_hbm.1, bf16[8,8192]{1,0:T(8,128)(2,1)} %wdt_ref.1, f32[8]{0:T(128)} %bias_ref.1, f32[8]{0:T(128)} %alog_ref.1, f32[8]{0:T(128)} %skip_ref.1, s32[8]{0:T(128)} %docs.1, ...), custom_call_target="tpu_custom_call" | custom-call | tf_op jit(solution)/shard_map/layer/pallas_call | solution.py:650
  79.9 0.7 copy.12
  80.6 0.7 copy.13

commit v4 on v3

--- a/solution.py
+++ b/solution.py
@@ -523,13 +523,33 @@
     own, sbs = xb.at[0:128, :], xb.at[128:256, :]
     for place in range(PLANES):
         for half in range(2):
-            at = half * 128 + SLOT[place] * 16
+            slot = SLOT[place]
+            if slot == 7:
+                at = half * 16
+            elif slot >= 5:
+                at = 32 + half * 32 + (slot - 5) * 16
+            else:
+                at = 96 + half * 80 + slot * 16
             pga[at : at + 16, :] = pgn[home(place, half), :]
 
-    def multiply(quarter):
-        term = mm(pga[...], wt[:, cols(quarter)]).astype(BF)
-        own[:, cols(quarter)] = term[0:128]
-        sbs[:, cols(quarter)] = term[128:256]
+    def multiply(quarter, begin, first, last):
+        count = last - first
+        rows = pga[begin : begin + 2 * count, :]
+        term = mm(rows, wt[:, cols(quarter)]).astype(BF)
+        own[first:last, cols(quarter)] = term[0:count]
+        sbs[first:last, cols(quarter)] = term[count : 2 * count]
+
+    def multiply_far(quarter):
+        multiply(quarter, 0, 112, 128)
+        swap_far(quarter).start()
+
+    def multiply_next(quarter):
+        multiply(quarter, 32, 80, 112)
+        swap_next(quarter).start()
+
+    def multiply_rest(quarter):
+        multiply(quarter, 96, 0, 80)
+        swap_rest(quarter).start()
 
     def swap(quarter, first, last, sems):
         return pltpu.make_async_remote_copy(
@@ -569,77 +589,78 @@
         where = cols(quarter, count)
         return own[at, where].astype(F32) + sbr[at, where].astype(F32)
 
-    def go_up(step, quarter, count):
-        value = pair_sum(4 - step, quarter, count)
-        if step > 1 or (step == 1 and quarter == 0):
-            for unit in quarters[:2] if step == 1 else ((quarter, count),):
-                pass_up(step - 1, *unit).wait_recv()
-            value = value + ru_r[step - 1, :, cols(quarter, count)].astype(F32)
-        own[place_rows(4 - step), cols(quarter, count)] = value.astype(BF)
-        pass_up(step, quarter, count).start()
-
-    def go_down(step, quarter, count):
-        value = pair_sum(4 + step, quarter, count)
-        if step > 1 or (step == 1 and quarter == 2):
-            for unit in quarters[2:] if step == 1 else ((quarter, count),):
-                pass_down(step - 1, *unit).wait_recv()
-            value = value + rd_r[step - 1, :, cols(quarter, count)].astype(F32)
-        own[place_rows(4 + step), cols(quarter, count)] = value.astype(BF)
-        pass_down(step, quarter, count).start()
+    def go_up(step, quarter):
+        value = pair_sum(4 - step, quarter, 1)
+        if step > 1 or (step == 1 and quarter < 2):
+            pass_up(step - 1, quarter, 1).wait_recv()
+            value = value + ru_r[step - 1, :, cols(quarter)].astype(F32)
+        own[place_rows(4 - step), cols(quarter)] = value.astype(BF)
+        pass_up(step, quarter, 1).start()
+
+    def go_down(step, quarter):
+        value = pair_sum(4 + step, quarter, 1)
+        if step > 1 or (step == 1 and quarter >= 2):
+            pass_down(step - 1, quarter, 1).wait_recv()
+            value = value + rd_r[step - 1, :, cols(quarter)].astype(F32)
+        own[place_rows(4 + step), cols(quarter)] = value.astype(BF)
+        pass_down(step, quarter, 1).start()
 
     def first_pass(quarter):
         swap_far(quarter).wait_recv()
-        (go_up if quarter < 2 else go_down)(0, quarter, 1)
+        (go_up if quarter < 2 else go_down)(0, quarter)
 
     for quarter in (0, 2, 1, 3):
-        multiply(quarter)
-        swap_far(quarter).start()
-        swap_next(quarter).start()
-    for quarter in (0, 2, 1, 3):
-        swap_rest(quarter).start()
-    for quarter in (0, 2, 1, 3):
-        first_pass(quarter)
-    for quarter in (2, 3):
-        swap_next(quarter).wait_recv()
-    go_up(1, 2, 2)
-    for quarter in (0, 1):
-        swap_next(quarter).wait_recv()
-    go_down(1, 0, 2)
-    go_up(1, 0, 2)
-    go_down(1, 2, 2)
-    for quarter in range(4):
-        swap_rest(quarter).wait_recv()
-    y_out[...] = yn[...].astype(BF)
-    for step in (2, 3):
-        go_up(step, 2, 2)
-        go_down(step, 0, 2)
-        go_up(step, 0, 2)
-        go_down(step, 2, 2)
-
-    def finish(quarter, up_here, down_here):
-        value = pair_sum(0, quarter, 2)
-        if up_here:
-            pass_up(3, quarter, 2).wait_recv()
-        if down_here:
-            pass_down(3, quarter, 2).wait_recv()
-        value = value + ru_r[3, :, cols(quarter, 2)].astype(F32)
-        value = value + rd_r[3, :, cols(quarter, 2)].astype(F32)
-        gh_out[:, cols(quarter, 2)] = value.astype(BF)
-
-    finish(2, True, True)
-    finish(0, True, True)
+        multiply_far(quarter)
+    for quarter, ready in ((2, 0), (0, 2), (3, 1), (1, 3)):
+        multiply_next(quarter)
+        first_pass(ready)
+    up_order, down_order = (2, 3, 0, 1), (0, 1, 2, 3)
+    seen = set()
+    for step in (1, 2, 3):
+        for up_quarter, down_quarter in zip(up_order, down_order):
+            for quarter in (up_quarter, down_quarter):
+                if step == 1 and quarter not in seen:
+                    swap_next(quarter).wait_recv()
+                    seen.add(quarter)
+            go_up(step, up_quarter)
+            go_down(step, down_quarter)
+            if step == 1:
+                multiply_rest(up_quarter)
+        if step == 1:
+            for quarter in range(4):
+                swap_rest(quarter).wait_recv()
+            y_out[...] = yn[...].astype(BF)
+
+    for up_quarter, down_quarter in zip(up_order, down_order):
+        pass_up(3, up_quarter, 1).wait_recv()
+        pass_down(3, down_quarter, 1).wait_recv()
+        if up_quarter < 2:
+            for quarter in (up_quarter, down_quarter):
+                value = pair_sum(0, quarter, 1)
+                value = value + ru_r[3, :, cols(quarter)].astype(F32)
+                value = value + rd_r[3, :, cols(quarter)].astype(F32)
+                gh_out[:, cols(quarter)] = value.astype(BF)
 
     for quarter in range(4):
         swap_far(quarter).wait_send()
         swap_next(quarter).wait_send()
         swap_rest(quarter).wait_send()
     for step in range(4):
-        for unit in quarters[:2] if step == 0 else halves:
+        for unit in quarters[:2] if step == 0 else quarters:
             pass_up(step, *unit).wait_send()
-        for unit in quarters[2:] if step == 0 else halves:
+        for unit in quarters[2:] if step == 0 else quarters:
             pass_down(step, *unit).wait_send()
     every(lambda step: out1(step).wait_send())
     every(lambda step: out2(step).wait_send())
+
+
+def place_results(y_in, gh_in, y_out, gh_out, sems):
+    y_copy = pltpu.make_async_copy(y_in, y_out, sems.at[0])
+    gh_copy = pltpu.make_async_copy(gh_in, gh_out, sems.at[1])
+    gh_copy.start()
+    y_copy.start()
+    gh_copy.wait()
+    y_copy.wait()
 
 
 def per_device(hidden, w_proj, w_dt, dt_bias, a_log, d_skip, doc_lengths, grad_out):
@@ -647,7 +668,7 @@
     smem = pl.BlockSpec(memory_space=pltpu.SMEM)
     dma = pltpu.SemaphoreType.DMA
     whole = pl.BlockSpec(memory_space=pl.ANY)
-    return pl.pallas_call(
+    results = pl.pallas_call(
         kernel,
         out_shape=(
             pltpu.VMEM((SPAN, XW), BF),
@@ -704,6 +725,17 @@
         ),
         name="layer",
     )(hidden, w_proj, w_dt, dt_bias, a_log, d_skip, doc_lengths, grad_out)
+    return pl.pallas_call(
+        place_results,
+        out_shape=(
+            jax.ShapeDtypeStruct((SPAN, XW), BF),
+            jax.ShapeDtypeStruct((ROWS, FEAT), BF),
+        ),
+        in_specs=[vmem, vmem],
+        out_specs=(whole, whole),
+        scratch_shapes=[dma((2,))],
+        name="place_results",
+    )(*(pltpu.with_memory_space_constraint(part, pltpu.VMEM) for part in results))
 
 
 def solution(mesh):

time: 81.4 us -> 80.1 us (0.984)
  local copies, waits for them, and re-layouts: 1.41 us -> 0 us
    unnamed x2 -> x0, local copies, waits for them, and re-layouts: 1.41 us -> none
    pallas_call x1, Pallas kernels: 79.3 us -> 78.3 us  [per_device(): pl.pallas_call(kernel, out_shape=(pltpu.VMEM((SPAN, XW), BF), pltpu.VMEM(...]
where the time goes in v4:
time: 80.1 us; the launch traced here: 79.9 us
  Pallas kernels  79.1 us (99%)
    pallas_call x1, Pallas kernels, per_device(): pl.pallas_call(kernel, out_shape=(pltpu.VMEM((SPAN, XW), BF), pltpu.VMEM(...  78.3 us

profile of v4, /device:TPU:1, one launch (start us, length us, event | category | flops | bytes accessed | tf_op | source)
XLA Modules:
  0.0 79.9 jit_solution(11082223529815353515)
XLA Ops:
  0.6 78.3 %layer.1 = (bf16[256,512]{1,0:T(8,128)(2,1)S(1)}, bf16[16,8192]{1,0:T(8,128)(2,1)S(1)}) custom-call(bf16[16,8192]{1,0:T(8,128)(2,1)} %hid.1, bf16[8192,768]{1,0:T(8,128)(2,1)} %w_hbm.1, bf16[8,8192]{1,0:T(8,128)(2,1)} %wdt_ref.1, f32[8]{0:T(128)} %bias_ref.1, f32[8]{0:T(128)} %alog_ref.1, f32[8]{0:T(128)} %skip_ref.1, s32[8]{0:T(128)} %docs.1, ...), custom_call_target="tpu_custom_call" | custom-call | tf_op jit(solution)/shard_map/layer/pallas_call | solution.py:671
  79.0 0.8 %place_results.1 = (bf16[256,512]{1,0:T(8,128)(2,1)}, bf16[16,8192]{1,0:T(8,128)(2,1)}) custom-call(bf16[256,512]{1,0:T(8,128)(2,1)S(1)} %get-tuple-element.4.y_in, bf16[16,8192]{1,0:T(8,128)(2,1)S(1)} %get-tuple-element.5.gh_in), custom_call_target="tpu_custom_call" | custom-call | tf_op jit(solution)/shard_map/place_results/pallas_call | solution.py:728

commit v5 on v4

--- a/solution.py
+++ b/solution.py
@@ -97,8 +97,9 @@
 
 
 def kernel(
-    hid, w_hbm, wdt_ref, bias_ref, alog_ref, skip_ref, docs, go,
+    hid_hbm, w_hbm, wdt_hbm, bias_hbm, alog_hbm, skip_hbm, docs_hbm, go_hbm,
     y_out, gh_out,
+    hid, wdt_ref, go, bias_ref, alog_ref, skip_ref, docs, in_sems,
     w, wt, xb, acc, bias_m, masks, spreader, gyt, pn, dn_, xn, dstn, bc, dte, kdd, crw, xk, ku, gw,
     ut, yt, dut, ds_, yn, pre, dbc, xs, xr, os_, or_, pgn, pga, sbr, ru_r, rd_r,
     wsem, au_s, au_r, ad_s, ad_r, ab_s, ab_r, x1s, x1r, x2s, x2r,
@@ -112,8 +113,8 @@
     down = lax.rem(z + PLANES - 1, PLANES) * 2 + core
     twin = z * 2 + (1 - core)
 
-    w_copy = pltpu.make_async_copy(w_hbm, w.at[:, 0:PROJ], wsem)
-    w_copy.start()
+    hid_copy = pltpu.make_async_copy(hid_hbm, hid, in_sems.at[0])
+    hid_copy.start()
 
     barrier = pltpu.get_barrier_semaphore()
     for near in (up, down, twin):
@@ -173,6 +174,24 @@
         )
         xb[0:ROWS, quarter * QUARTER : (quarter + 1) * QUARTER] = flat.astype(BF)
 
+    later_copies = [
+        pltpu.make_async_copy(source, target, in_sems.at[1 + at])
+        for at, (source, target) in enumerate(
+            (
+                (docs_hbm, docs),
+                (wdt_hbm, wdt_ref),
+                (go_hbm, go),
+                (bias_hbm, bias_ref),
+                (alog_hbm, alog_ref),
+                (skip_hbm, skip_ref),
+            )
+        )
+    ]
+    for copy in later_copies:
+        copy.start()
+    w_copy = pltpu.make_async_copy(w_hbm, w.at[:, 0:PROJ], wsem)
+    w_copy.start()
+    hid_copy.wait()
     encode(0)
     pl.semaphore_wait(barrier, 7)
     to_up(0, 0, 1).start()
@@ -189,6 +208,8 @@
     to_twin(0, 0, 4).start()
     tell(beside, heard.at[0])
 
+    for copy in later_copies:
+        copy.wait()
     first_token = span * SPAN
 
     def segment(positions):
@@ -665,7 +686,6 @@
 
 def per_device(hidden, w_proj, w_dt, dt_bias, a_log, d_skip, doc_lengths, grad_out):
     vmem = pl.BlockSpec(memory_space=pltpu.VMEM)
-    smem = pl.BlockSpec(memory_space=pltpu.SMEM)
     dma = pltpu.SemaphoreType.DMA
     whole = pl.BlockSpec(memory_space=pl.ANY)
     results = pl.pallas_call(
@@ -674,9 +694,17 @@
             pltpu.VMEM((SPAN, XW), BF),
             pltpu.VMEM((ROWS, FEAT), BF),
         ),
-        in_specs=[vmem, whole, vmem, smem, smem, smem, smem, vmem],
+        in_specs=[whole] * 8,
         out_specs=(vmem, vmem),
         scratch_shapes=[
+            pltpu.VMEM((ROWS, FEAT), BF),
+            pltpu.VMEM((HEADS, FEAT), BF),
+            pltpu.VMEM((SPAN, XW), BF),
+            pltpu.SMEM((HEADS,), F32),
+            pltpu.SMEM((HEADS,), F32),
+            pltpu.SMEM((HEADS,), F32),
+            pltpu.SMEM((8,), jnp.int32),
+            dma((7,)),
             pltpu.VMEM((FEAT, WIDE), BF),
             pltpu.VMEM((WIDE, FEAT), BF),
             pltpu.VMEM((SPAN, FEAT), BF),

time: 80.1 us -> 79 us (0.986)
  Pallas kernels: 79.1 us -> 78.1 us
    pallas_call x1, Pallas kernels: 78.3 us -> 77.3 us  [per_device(): pl.pallas_call(kernel, out_shape=(pltpu.VMEM((SPAN, XW), BF), pltpu.VMEM(...]
where the time goes in v5:
time: 79 us; the launch traced here: 78.9 us
  Pallas kernels  78.1 us (99%)
  between operations  0.8 us (1%)
    pallas_call x1, Pallas kernels, per_device(): pl.pallas_call(kernel, out_shape=(pltpu.VMEM((SPAN, XW), BF), pltpu.VMEM(...  77.3 us

profile of v5, /device:TPU:1, one launch (start us, length us, event | category | flops | bytes accessed | tf_op | source)
XLA Modules:
  0.0 78.9 jit_solution(2100200733713861560)
XLA Ops:
  0.6 77.3 %layer.1 = (bf16[256,512]{1,0:T(8,128)(2,1)S(1)}, bf16[16,8192]{1,0:T(8,128)(2,1)S(1)}) custom-call(bf16[16,8192]{1,0:T(8,128)(2,1)} %hid_hbm.1, bf16[8192,768]{1,0:T(8,128)(2,1)} %w_hbm.1, bf16[8,8192]{1,0:T(8,128)(2,1)} %wdt_hbm.1, f32[8]{0:T(128)} %bias_hbm.1, f32[8]{0:T(128)} %alog_hbm.1, f32[8]{0:T(128)} %skip_hbm.1, s32[8]{0:T(128)} %docs_hbm.1, ...), custom_call_target="tpu_custom_call" | custom-call | tf_op jit(solution)/shard_map/layer/pallas_call | solution.py:691
  77.9 0.8 %place_results.1 = (bf16[256,512]{1,0:T(8,128)(2,1)}, bf16[16,8192]{1,0:T(8,128)(2,1)}) custom-call(bf16[256,512]{1,0:T(8,128)(2,1)S(1)} %get-tuple-element.4.y_in, bf16[16,8192]{1,0:T(8,128)(2,1)S(1)} %get-tuple-element.5.gh_in), custom_call_target="tpu_custom_call" | custom-call | tf_op jit(solution)/shard_map/place_results/pallas_call | solution.py:756

commit v6 on v5

--- a/solution.py
+++ b/solution.py
@@ -97,9 +97,9 @@
 
 
 def kernel(
-    hid_hbm, w_hbm, wdt_hbm, bias_hbm, alog_hbm, skip_hbm, docs_hbm, go_hbm,
+    hid_hbm, w_hbm, wdt_ref, bias_hbm, alog_hbm, skip_hbm, docs_hbm, go_hbm,
     y_out, gh_out,
-    hid, wdt_ref, go, bias_ref, alog_ref, skip_ref, docs, in_sems,
+    hid, go, bias_ref, alog_ref, skip_ref, docs, in_sems,
     w, wt, xb, acc, bias_m, masks, spreader, gyt, pn, dn_, xn, dstn, bc, dte, kdd, crw, xk, ku, gw,
     ut, yt, dut, ds_, yn, pre, dbc, xs, xr, os_, or_, pgn, pga, sbr, ru_r, rd_r,
     wsem, au_s, au_r, ad_s, ad_r, ab_s, ab_r, x1s, x1r, x2s, x2r,
@@ -179,7 +179,6 @@
         for at, (source, target) in enumerate(
             (
                 (docs_hbm, docs),
-                (wdt_hbm, wdt_ref),
                 (go_hbm, go),
                 (bias_hbm, bias_ref),
                 (alog_hbm, alog_ref),
@@ -694,17 +693,16 @@
             pltpu.VMEM((SPAN, XW), BF),
             pltpu.VMEM((ROWS, FEAT), BF),
         ),
-        in_specs=[whole] * 8,
+        in_specs=[whole, whole, vmem, whole, whole, whole, whole, whole],
         out_specs=(vmem, vmem),
         scratch_shapes=[
             pltpu.VMEM((ROWS, FEAT), BF),
-            pltpu.VMEM((HEADS, FEAT), BF),
             pltpu.VMEM((SPAN, XW), BF),
             pltpu.SMEM((HEADS,), F32),
             pltpu.SMEM((HEADS,), F32),
             pltpu.SMEM((HEADS,), F32),
             pltpu.SMEM((8,), jnp.int32),
-            dma((7,)),
+            dma((6,)),
             pltpu.VMEM((FEAT, WIDE), BF),
             pltpu.VMEM((WIDE, FEAT), BF),
             pltpu.VMEM((SPAN, FEAT), BF),

time: 79 us -> 79.9 us (1.011)
  Pallas kernels: 78.1 us -> 79 us
    pallas_call x1, Pallas kernels: 77.3 us -> 78.2 us  [per_device(): pl.pallas_call(kernel, out_shape=(pltpu.VMEM((SPAN, XW), BF), pltpu.VMEM(...]
where the time goes in v6:
time: 79.9 us; the launch traced here: 79.8 us
  Pallas kernels  79 us (99%)
  between operations  0.8 us (1%)
    pallas_call x1, Pallas kernels, per_device(): pl.pallas_call(kernel, out_shape=(pltpu.VMEM((SPAN, XW), BF), pltpu.VMEM(...  78.2 us

profile of v6, /device:TPU:1, one launch (start us, length us, event | category | flops | bytes accessed | tf_op | source)
XLA Modules:
  0.0 79.8 jit_solution(15127041358502294882)
XLA Ops:
  0.6 78.2 %layer.1 = (bf16[256,512]{1,0:T(8,128)(2,1)S(1)}, bf16[16,8192]{1,0:T(8,128)(2,1)S(1)}) custom-call(bf16[16,8192]{1,0:T(8,128)(2,1)} %hid_hbm.1, bf16[8192,768]{1,0:T(8,128)(2,1)} %w_hbm.1, bf16[8,8192]{1,0:T(8,128)(2,1)} %wdt_ref.1, f32[8]{0:T(128)} %bias_hbm.1, f32[8]{0:T(128)} %alog_hbm.1, f32[8]{0:T(128)} %skip_hbm.1, s32[8]{0:T(128)} %docs_hbm.1, ...), custom_call_target="tpu_custom_call" | custom-call | tf_op jit(solution)/shard_map/layer/pallas_call | solution.py:690
  78.8 0.8 %place_results.1 = (bf16[256,512]{1,0:T(8,128)(2,1)}, bf16[16,8192]{1,0:T(8,128)(2,1)}) custom-call(bf16[256,512]{1,0:T(8,128)(2,1)S(1)} %get-tuple-element.4.y_in, bf16[16,8192]{1,0:T(8,128)(2,1)S(1)} %get-tuple-element.5.gh_in), custom_call_target="tpu_custom_call" | custom-call | tf_op jit(solution)/shard_map/place_results/pallas_call | solution.py:754
